TPU v7x, 32 devices: a whole 2x2x4 slice. The times are simulated.
32 devices in a mesh: ctx: 8 (over z, y), ch: 4 (over x, core).
Axes of the slice: x: 2, y: 2, z: 4, core: 2. Of those that a mesh axis runs over, the one named last changes fastest.
Arguments:
- query_input: bfloat16 [4096, 2048], P('ctx', 'ch'), may hold values from -6 to 6
- key_input: bfloat16 [4096, 2048], P('ctx', 'ch'), may hold values from -6 to 6
- value_input: bfloat16 [4096, 2048], P('ctx', 'ch'), may hold values from -6 to 6
- filters: bfloat16 [2, 4096], replicated, may hold values from -1 to 1
- cotangent: bfloat16 [4096, 2048], P('ctx', 'ch'), may hold values from -6 to 6
Outputs:
- query_adjoint: bfloat16 [4096, 2048], P('ctx', 'ch')
- key_adjoint: bfloat16 [4096, 2048], P('ctx', 'ch')
- value_adjoint: bfloat16 [4096, 2048], P('ctx', 'ch')
- filter_adjoint: float32 [2, 4096], P(None, 'ctx')
All inputs are finite; a program needn't handle non-finite values.
Results may differ from a plain program's by a relative error of at most 0.0051.
Values may be sent and summed in bfloat16 or wider, within the bound.
No kernel may reach another device: no remote copies, remote signals or barrier semaphores. Data moves between devices by JAX's collectives and lax.ppermute only.
A program may use at most 64 MiB of HBM per device.

v0:
```python
import math

import jax
import jax.numpy as jnp
from jax import lax
from jax.sharding import PartitionSpec as P

GW = 1024


def toeplitz_tile(padded_taps, offset, side_len):
    window = lax.dynamic_slice_in_dim(padded_taps, offset + 1, 2 * side_len)
    pattern = jnp.concatenate([window[:side_len][::-1], window[side_len:][::-1]])
    repeated = jnp.tile(pattern, side_len)[: side_len * (2 * side_len - 1)]
    return repeated.reshape(side_len, 2 * side_len - 1)[:, :side_len]


def lag_sums(cross_prod):
    side_len = cross_prod.shape[0]
    padded = jnp.pad(cross_prod[:, ::-1], ((0, 0), (0, side_len)))
    sheared = padded.reshape(-1)[: side_len * (2 * side_len - 1)].reshape(
        side_len, 2 * side_len - 1
    )
    return jnp.sum(sheared, axis=0)


def add_lags(lag_total, cross_prod, offset):
    side_len = cross_prod.shape[0]
    previous = lax.dynamic_slice_in_dim(lag_total, offset + 1, 2 * side_len - 1)
    return lax.dynamic_update_slice_in_dim(
        lag_total, previous + lag_sums(cross_prod), offset + 1, 0
    )


def apply_transpose(band_tile, block_rows):
    return lax.dot_general(
        band_tile, block_rows, (((0,), (0,)), ((), ())), preferred_element_type=jnp.float32
    )


def cross_rows(left_rows, right_rows):
    return lax.dot_general(
        left_rows, right_rows, (((1,), (1,)), ((), ())), preferred_element_type=jnp.float32
    )


def elementwise(left_arr, right_arr):
    return (left_arr.astype(jnp.float32) * right_arr.astype(jnp.float32)).astype(jnp.bfloat16)


def on_device(query_input, key_input, value_input, filters, cotangent):
    tok_rows, channels = query_input.shape
    num_groups, seq_total = filters.shape
    group_index = lax.axis_index("ch") * channels // GW
    filter_taps = lax.dynamic_index_in_dim(filters, group_index, 0, keepdims=False)
    zero_rows = jnp.zeros((tok_rows,), filters.dtype)
    padded_taps = jnp.concatenate([zero_rows, filter_taps, zero_rows])
    lag_init = jnp.zeros((seq_total + 2 * tok_rows,), jnp.float32)
    product = elementwise(key_input, value_input)
    gated_adj = elementwise(cotangent, query_input)
    row_start = lax.axis_index("ctx") * tok_rows

    def fold_active(loop_state, key_block, offset):
        mixed_rows, lag_total = loop_state
        band_tile = toeplitz_tile(padded_taps, offset, tok_rows)
        mixed_rows = mixed_rows + jnp.dot(band_tile, key_block, preferred_element_type=jnp.float32)
        lag_total = add_lags(lag_total, cross_rows(gated_adj, key_block), offset)
        return (mixed_rows, lag_total)

    def fold_skip(loop_state, key_block, offset):
        return loop_state

    mixed_init = jnp.zeros((tok_rows, channels), jnp.float32)
    gathered = lax.all_gather(product, "ctx", axis=0, tiled=True)

    def forward_one_block(sub_block, loop_state):
        key_block = lax.dynamic_slice_in_dim(gathered, sub_block * tok_rows, tok_rows, 0)
        offset = row_start - sub_block * tok_rows
        return lax.cond(offset >= 0, fold_active, fold_skip, loop_state, key_block, offset)

    mixed_rows, lag_total = lax.fori_loop(
        0, gathered.shape[0] // tok_rows, forward_one_block, (mixed_init, lag_init)
    )

    def back_active(loop_state, adj_block, offset):
        return loop_state + apply_transpose(toeplitz_tile(padded_taps, offset, tok_rows), adj_block)

    def back_skip(loop_state, adj_block, offset):
        return loop_state

    backward_gathered = lax.all_gather(gated_adj, "ctx", axis=0, tiled=True)

    def backward_one_block(sub_block, loop_state):
        adj_block = lax.dynamic_slice_in_dim(backward_gathered, sub_block * tok_rows, tok_rows, 0)
        offset = sub_block * tok_rows - row_start
        return lax.cond(offset >= 0, back_active, back_skip, loop_state, adj_block, offset)

    back_rows = lax.fori_loop(
        0, backward_gathered.shape[0] // tok_rows, backward_one_block, mixed_init
    )
    query_adjoint = (cotangent.astype(jnp.float32) * mixed_rows).astype(jnp.bfloat16)
    key_adjoint = (back_rows * value_input.astype(jnp.float32)).astype(jnp.bfloat16)
    value_adjoint = (back_rows * key_input.astype(jnp.float32)).astype(jnp.bfloat16)
    lag_vector = lag_total[tok_rows : tok_rows + seq_total] * (1.0 / math.sqrt(seq_total * GW))
    spread = jnp.where(
        jnp.arange(num_groups, dtype=jnp.int32)[:, None] == group_index,
        lag_vector[None, :],
        jnp.float32(0.0),
    )
    summed = lax.psum(spread, ("ctx", "ch"))
    filter_adjoint = lax.dynamic_slice_in_dim(summed, lax.axis_index("ctx") * tok_rows, tok_rows, 1)
    return (query_adjoint, key_adjoint, value_adjoint, filter_adjoint)


def solution(mesh):
    return jax.shard_map(
        on_device,
        mesh=mesh,
        in_specs=(P("ctx", "ch"), P("ctx", "ch"), P("ctx", "ch"), P(), P("ctx", "ch")),
        out_specs=(P("ctx", "ch"), P("ctx", "ch"), P("ctx", "ch"), P(None, "ctx")),
        check_vma=False,
    )
```

profile of v0, /device:TPU:0, one launch (start us, length us, event | category | flops | bytes accessed | tf_op | source)
XLA Modules:
  0.0 335.1 jit_solution(14521042344463210715)
XLA Ops:
  7.2 2.1 fusion.8
  9.6 77.3 %all-gather.5.cloned.1.call-done = bf16[4096,512]{1,0:T(8,128)(2,1)} async-done(((bf16[512,512]{1,0:T(8,128)(2,1)}), bf16[4096,512]{1,0:T(8,128)(2,1)}) %all-gather.5.cloned.1.call-update) | async-done | bytes 4194320 | tf_op jit(solution)/shard_map/all_gather | solution.py:91
  87.0 32.4 %while.32 = (s32[]{:T(128)}, f32[512,512]{1,0:T(8,128)S(1)}, s32[]{:T(128)}, bf16[5120]{0:T(1024)(128)(2,1)S(1)}, bf16[4096,512]{1,0:T(8,128)(2,1)}, /*index=5*/s32[]{:T(128)}, s32[]{:T(128)}, s32[]{:T(128)}) while((s32[]{:T(128)}, f32[512,512]{1,0:T(8,128)S(1)}, s32[]{:T(128)}, bf16[5120]{0:T(1024)(128)(2,1)S(1)}, ...), condition=%wide.region_8.9_spmd, body=%wide.region_5.8_spmd.sunk | while | flops 268701696 | bytes 8405251 | solution.py:98
  87.0 4.0 %conditional.5 = (f32[512,512]{1,0:T(8,128)S(1)}) conditional(s32[]{:T(128)} %convert_element_type.82, f32[512,512]{1,0:T(8,128)S(1)} %get-tuple-element.458, (s32[]{:T(128)}, bf16[5120]{0:T(1024)(128)(2,1)S(1)}, s32[]{:T(128)}, bf16[4096,512]{1,0:T(8,128)(2,1)}, f32[512,512]{1,0:T(8,128)S(1)}) %tuple.87), branch_computations={%region_6.6_spmd, %region_7.7_spmd} | conditional | flops 268701696 | bytes 8405088 | solution.py:96
  87.8 1.6 reshape.31
  91.0 4.0 %conditional.5 = (f32[512,512]{1,0:T(8,128)S(1)}) conditional(s32[]{:T(128)} %convert_element_type.82, f32[512,512]{1,0:T(8,128)S(1)} %get-tuple-element.458, (s32[]{:T(128)}, bf16[5120]{0:T(1024)(128)(2,1)S(1)}, s32[]{:T(128)}, bf16[4096,512]{1,0:T(8,128)(2,1)}, f32[512,512]{1,0:T(8,128)S(1)}) %tuple.87), branch_computations={%region_6.6_spmd, %region_7.7_spmd} | conditional | flops 268701696 | bytes 8405088 | solution.py:96
  91.9 1.6 reshape.31
  95.1 4.0 %conditional.5 = (f32[512,512]{1,0:T(8,128)S(1)}) conditional(s32[]{:T(128)} %convert_element_type.82, f32[512,512]{1,0:T(8,128)S(1)} %get-tuple-element.458, (s32[]{:T(128)}, bf16[5120]{0:T(1024)(128)(2,1)S(1)}, s32[]{:T(128)}, bf16[4096,512]{1,0:T(8,128)(2,1)}, f32[512,512]{1,0:T(8,128)S(1)}) %tuple.87), branch_computations={%region_6.6_spmd, %region_7.7_spmd} | conditional | flops 268701696 | bytes 8405088 | solution.py:96
  96.0 1.6 reshape.31
  99.2 4.0 %conditional.5 = (f32[512,512]{1,0:T(8,128)S(1)}) conditional(s32[]{:T(128)} %convert_element_type.82, f32[512,512]{1,0:T(8,128)S(1)} %get-tuple-element.458, (s32[]{:T(128)}, bf16[5120]{0:T(1024)(128)(2,1)S(1)}, s32[]{:T(128)}, bf16[4096,512]{1,0:T(8,128)(2,1)}, f32[512,512]{1,0:T(8,128)S(1)}) %tuple.87), branch_computations={%region_6.6_spmd, %region_7.7_spmd} | conditional | flops 268701696 | bytes 8405088 | solution.py:96
  103.2 4.0 %conditional.5 = (f32[512,512]{1,0:T(8,128)S(1)}) conditional(s32[]{:T(128)} %convert_element_type.82, f32[512,512]{1,0:T(8,128)S(1)} %get-tuple-element.458, (s32[]{:T(128)}, bf16[5120]{0:T(1024)(128)(2,1)S(1)}, s32[]{:T(128)}, bf16[4096,512]{1,0:T(8,128)(2,1)}, f32[512,512]{1,0:T(8,128)S(1)}) %tuple.87), branch_computations={%region_6.6_spmd, %region_7.7_spmd} | conditional | flops 268701696 | bytes 8405088 | solution.py:96
  107.3 4.0 %conditional.5 = (f32[512,512]{1,0:T(8,128)S(1)}) conditional(s32[]{:T(128)} %convert_element_type.82, f32[512,512]{1,0:T(8,128)S(1)} %get-tuple-element.458, (s32[]{:T(128)}, bf16[5120]{0:T(1024)(128)(2,1)S(1)}, s32[]{:T(128)}, bf16[4096,512]{1,0:T(8,128)(2,1)}, f32[512,512]{1,0:T(8,128)S(1)}) %tuple.87), branch_computations={%region_6.6_spmd, %region_7.7_spmd} | conditional | flops 268701696 | bytes 8405088 | solution.py:96
  108.1 1.6 reshape.31
  111.3 4.0 %conditional.5 = (f32[512,512]{1,0:T(8,128)S(1)}) conditional(s32[]{:T(128)} %convert_element_type.82, f32[512,512]{1,0:T(8,128)S(1)} %get-tuple-element.458, (s32[]{:T(128)}, bf16[5120]{0:T(1024)(128)(2,1)S(1)}, s32[]{:T(128)}, bf16[4096,512]{1,0:T(8,128)(2,1)}, f32[512,512]{1,0:T(8,128)S(1)}) %tuple.87), branch_computations={%region_6.6_spmd, %region_7.7_spmd} | conditional | flops 268701696 | bytes 8405088 | solution.py:96
  115.4 4.0 %conditional.5 = (f32[512,512]{1,0:T(8,128)S(1)}) conditional(s32[]{:T(128)} %convert_element_type.82, f32[512,512]{1,0:T(8,128)S(1)} %get-tuple-element.458, (s32[]{:T(128)}, bf16[5120]{0:T(1024)(128)(2,1)S(1)}, s32[]{:T(128)}, bf16[4096,512]{1,0:T(8,128)(2,1)}, f32[512,512]{1,0:T(8,128)S(1)}) %tuple.87), branch_computations={%region_6.6_spmd, %region_7.7_spmd} | conditional | flops 268701696 | bytes 8405088 | solution.py:96
  119.4 2.6 fusion.10
  122.1 70.8 %all-gather.3.cloned.1.call-done = bf16[4096,512]{1,0:T(8,128)(2,1)} async-done(((bf16[512,512]{1,0:T(8,128)(2,1)}), bf16[4096,512]{1,0:T(8,128)(2,1)}) %all-gather.3.cloned.1.call-update) | async-done | bytes 4194320 | tf_op jit(solution)/shard_map/all_gather | solution.py:74
  193.0 12.2 %while.31 = (s32[]{:T(128)}, f32[512,512]{1,0:T(8,128)S(1)}, f32[5120]{0:T(1024)S(1)}, s32[]{:T(128)}, bf16[5120]{0:T(1024)(128)(2,1)S(1)}, /*index=5*/bf16[4096...) while((s32[]{:T(128)}, f32[512,512]{1,0:T(8,128)S(1)}, f32[5120]{0:T(1024)S(1)}, ...), condition=%wide.region_4.5_spmd, body=%wide.region_0.4_spmd.sunk | while | flops 537660928 | bytes 28338508 | solution.py:81
  193.0 12.0 %conditional.4 = ((f32[512,512]{1,0:T(8,128)S(1)}, f32[5120]{0:T(1024)S(1)})) conditional(s32[]{:T(128)} %convert_element_type.81, (f32[512,512]{1,0:T(8,128)S(1)}, f32[5120]{0:T(1024)S(1)}) %tuple.84, (s32[]{:T(128)}, bf16[5120]{0:T(1024)(128)(2,1)S(1)}, s32[]{:T(128)}, bf16[4096,512]{1,0:T(8,128)(2,1)}, f32[512,512]{1,0:T(8,128)S(1)}, ...), branch_computations={%region_1.1_spmd, %region_2.3_spmd} | conditional | flops 537660928 | bytes 28338296 | solution.py:79
  197.1 1.7 convolution_bitcast_fusion
  199.9 1.8 copy.13
  201.7 3.0 reshape.30
  205.2 2.0 fusion.9
  207.3 120.3 %psum.7 = f32[2,4096]{1,0:T(2,128)S(1)} all-reduce(f32[2,4096]{1,0:T(2,128)S(1)} %broadcast_select_fusion), channel_id=1, replica_groups=mesh['ctx'=8,'ch'=4] {'ctx','ch'}, use_global_device_ids=true, to_apply=%region_9.10 | all-reduce | flops 8192 | bytes 65536 | tf_op jit(solution)/shard_map/psum | solution.py:110
  (105 shorter events, 31.9 us)
Async XLA Ops:
  7.2 2.3 copy-start
  7.2 79.7 %all-gather.5.cloned.1.call-start = ((), (), s32[]{:S(2)}) async-start(), calls=%async_computation.1 | async-start | bytes 4718592 | tf_op jit(solution)/shard_map/all_gather | solution.py:91
  9.4 183.5 %all-gather.3.cloned.1.call-start = ((), (), s32[]{:S(2)}) async-start(), calls=%async_computation | async-start | bytes 4718592 | tf_op jit(solution)/shard_map/all_gather | solution.py:74
Sparse Core Ops, SparseCore 0:
  10.7 76.0 all-gather.4
  122.2 70.6 all-gather.2
where the time goes:
time: 336 us; the launch traced here: 335 us
  waiting for transfers between devices  148 us (44%)
  blocking collectives  120 us (36%)
  local copies, waits for them, and re-layouts  28.7 us (9%)
  matrix products  15.4 us (5%)
  between operations  14.1 us (4%)
  other arithmetic  7.32 us (2%)
    psum x1, blocking collectives, on_device(): summed = lax.psum(spread, ('ctx', 'ch'))  120 us
    all_gather x1, waiting for transfers between devices, on_device(): backward_gathered = lax.all_gather(gated_adj, 'ctx', axis=0, tiled=True)  77.3 us
    all_gather x1, waiting for transfers between devices, on_device(): gathered = lax.all_gather(product, 'ctx', axis=0, tiled=True)  70.8 us
    reshape x9, local copies, waits for them, and re-layouts, toeplitz_tile(): return repeated.reshape(side_len, 2 * side_len - 1)[:, :side_len]  14.7 us
    dot_general x8, matrix products, apply_transpose(): lax.dot_general(band_tile, block_rows, (((0,), (0,)), ((), ())), preferre...  12.2 us
    cond x21, local copies, waits for them, and re-layouts  7.03 us
  transfers between devices with their start and end apart: 2, of which 2 were waited for; matrix products, arithmetic and copies ran while one was open for 0% of the time, Pallas kernels for 0%

commit v1 on v0

v1 whole, which is shorter than its diff:
```python
import functools
import math

import jax
import jax.numpy as jnp
from jax import lax
from jax.experimental import pallas as pl
from jax.experimental.pallas import tpu as pltpu
from jax.sharding import PartitionSpec as P

GW = 1024
LANES = 128
VMEM_LIMIT = 56 * 1024 * 1024
VMEM = pl.BlockSpec(memory_space=pltpu.VMEM)
SMEM = pl.BlockSpec(memory_space=pltpu.SMEM)


def params():
    return pltpu.CompilerParams(vmem_limit_bytes=VMEM_LIMIT)


def f32_product(left, right):
    return left.astype(jnp.float32) * right.astype(jnp.float32)


def split_kernel(owners, place, key, value, query, cot, *outs):
    q, upper = place[0], place[1]
    for k in range(owners):
        lanes = pl.ds(pl.multiple_of((q ^ k) * LANES, LANES), LANES)
        product = f32_product(key[:, lanes], value[:, lanes]).astype(jnp.bfloat16)
        gated = f32_product(cot[:, lanes], query[:, lanes]).astype(jnp.bfloat16)
        outs[k][0] = product
        outs[k][1] = gated
        outs[owners + k][...] = jnp.where(upper == 1, gated, product)


def split_streams(owners, place, key, value, query, cot):
    rows, channels = key.shape
    width = channels // owners
    if width == LANES:
        pair = jax.ShapeDtypeStruct((2, rows, LANES), jnp.bfloat16)
        single = jax.ShapeDtypeStruct((rows, LANES), jnp.bfloat16)
        outs = pl.pallas_call(
            functools.partial(split_kernel, owners),
            out_shape=[pair] * owners + [single] * owners,
            in_specs=[SMEM] + [VMEM] * 4,
            out_specs=[VMEM] * (2 * owners),
            compiler_params=params(),
            name="split_streams",
        )(place, key, value, query, cot)
        return outs[:owners], outs[owners:]
    product = f32_product(key, value).astype(jnp.bfloat16)
    gated = f32_product(cot, query).astype(jnp.bfloat16)
    both = jnp.stack([product, gated]).reshape(2, rows, owners, width)
    both = jnp.pad(both, ((0, 0), (0, 0), (0, 0), (0, LANES - width)))
    pairs = [lax.dynamic_index_in_dim(both, place[0] ^ k, 2, keepdims=False) for k in range(owners)]
    return pairs, [jnp.where(place[1] == 1, pair[1], pair[0]) for pair in pairs]


def tables_kernel(rows_ref, out):
    block, seq = out.shape[1], out.shape[2]
    sub = lax.broadcasted_iota(jnp.int32, (8, rows_ref.shape[1]), 0)
    width = rows_ref.shape[1]
    for which in range(2):
        eight = jnp.broadcast_to(rows_ref[which : which + 1, :], (8, width))
        for bit in (1, 2, 4):
            eight = jnp.where((sub & bit) != 0, pltpu.roll(eight, bit, 1), eight)
        for pair in range(block // 16):
            low = pltpu.roll(eight, 16 * pair, 1) if pair else eight
            high = pltpu.roll(eight, 16 * pair + 8, 1)
            both = jnp.concatenate([low[:, :seq], high[:, :seq]], axis=0)
            out[which, 16 * pair : 16 * pair + 16, :] = both.astype(jnp.bfloat16)


def toeplitz_tables(taps, block):
    seq = taps.shape[0]
    zeros = jnp.zeros((block,), jnp.float32)
    taps = taps.astype(jnp.float32)
    down = jnp.concatenate([taps[::-1], zeros])
    down = jnp.concatenate([down[block - 1 :], down[: block - 1]])
    rows = jnp.stack([down, jnp.concatenate([taps, zeros])])
    return pl.pallas_call(
        tables_kernel,
        out_shape=jax.ShapeDtypeStruct((2, block, seq), jnp.bfloat16),
        in_specs=[VMEM],
        out_specs=VMEM,
        compiler_params=params(),
        name="toeplitz_tables",
    )(rows)


def lags_kernel(owners, place, *refs):
    halves, crossing = refs[:owners], refs[owners : 2 * owners]
    out, lane_blocks, sums = refs[2 * owners :]
    q, upper = place[0], place[1]
    block = halves[0].shape[1] // 2
    half_blocks = 2 * owners
    blocks = 2 * half_blocks
    lane_blocks[:, 2 * blocks * LANES :] = jnp.zeros((block, LANES), jnp.bfloat16)
    for k in range(owners):
        near = upper * half_blocks + 2 * (q ^ k)
        far = 2 * (q ^ k) + jnp.where(upper == 1, 0, blocks + half_blocks)
        for part in range(2):
            rows = slice(part * block, (part + 1) * block)
            for which in range(2):
                start = pl.multiple_of((near + which * blocks + part) * LANES, LANES)
                lane_blocks[:, pl.ds(start, LANES)] = halves[k][which, rows, :]
            start = pl.multiple_of((far + part) * LANES, LANES)
            lane_blocks[:, pl.ds(start, LANES)] = crossing[k][rows, :]
    for lag in range(blocks):
        count = (blocks - lag + 1) // 2
        first = jnp.where(upper == 1, count, 0)
        left = lane_blocks[:, pl.ds(pl.multiple_of(first * LANES, LANES), count * LANES)]
        start = pl.multiple_of((first + lag + blocks) * LANES, LANES)
        right = lane_blocks[:, pl.ds(start, count * LANES)]
        sums[lag] = lax.dot_general(
            left, right, (((1,), (1,)), ((), ())), preferred_element_type=jnp.float32
        )
    sums[blocks] = jnp.zeros((block, block), jnp.float32)
    steps = block // LANES

    def diagonal(lag):
        total = None
        for a in range(steps):
            b = lag + a
            rows = slice(a * LANES, (a + 1) * LANES)
            cols = slice((b % steps) * LANES, (b % steps + 1) * LANES)
            tile = sums[b // steps, rows, cols]
            total = tile if total is None else total + tile
        return total

    row = lax.broadcasted_iota(jnp.int32, (LANES, LANES), 0)
    col = lax.broadcasted_iota(jnp.int32, (LANES, LANES), 1)
    sub = lax.broadcasted_iota(jnp.int32, (8, LANES), 0)
    current = diagonal(0)
    for lag in range(steps * blocks):
        after = diagonal(lag + 1) if lag + 1 < steps * blocks else jnp.zeros_like(current)
        mixed = jnp.where(col >= row, current, after)
        eight = mixed[:8]
        for m in range(1, LANES // 8):
            eight = eight + pltpu.roll(mixed[8 * m : 8 * m + 8], LANES - 8 * m, 1)
        for bit in (1, 2, 4):
            eight = jnp.where((sub & bit) != 0, pltpu.roll(eight, LANES - bit, 1), eight)
        out[lag : lag + 1, :] = jnp.sum(eight, axis=0, keepdims=True)
        current = after


def lag_sums(owners, place, halves, crossing):
    block = halves[0].shape[1] // 2
    blocks = 4 * owners
    return pl.pallas_call(
        functools.partial(lags_kernel, owners),
        out_shape=jax.ShapeDtypeStruct((blocks * block // LANES, LANES), jnp.float32),
        in_specs=[SMEM] + [VMEM] * (2 * owners),
        out_specs=VMEM,
        scratch_shapes=[
            pltpu.VMEM((block, (2 * blocks + 1) * LANES), jnp.bfloat16),
            pltpu.VMEM((blocks + 1, block, block), jnp.float32),
        ],
        compiler_params=params(),
        name="lag_sums",
    )(place, *halves, *crossing)


def conv_kernel(owners, place, tables, *refs):
    halves, crossing = refs[:owners], refs[owners : 2 * owners]
    outs = refs[2 * owners : 3 * owners]
    whole, half, results = refs[3 * owners :]
    q, upper = place[0], place[1]
    rows = halves[0].shape[1]
    block = rows // 2
    half_blocks = 2 * owners
    blocks = 2 * half_blocks
    zeros = jnp.zeros((block, LANES), jnp.bfloat16)
    for ref, count in ((whole, blocks), (half, half_blocks)):
        ref[:block] = zeros
        ref[(count + 1) * block :] = zeros
    for k in range(owners):
        start = block + (q ^ k) * rows
        near = pl.multiple_of(start + upper * half_blocks * block, block)
        far = pl.multiple_of(start + (1 - upper) * half_blocks * block, block)
        own, other = halves[k][1 - upper], halves[k][upper]
        whole[pl.ds(near, rows), :] = own
        whole[pl.ds(far, rows), :] = crossing[k][...]
        half[pl.ds(pl.multiple_of(start, block), rows), :] = other
    for ref, count, table, slot in (
        (whole, half_blocks, 1 - upper, 1 - upper),
        (half, 0, upper, upper),
    ):
        for i in range(owners):
            depth = (count + 2 * i + 2) * block
            down = (blocks * block - depth) * (1 - table)
            first = table * (half_blocks - 1 - 2 * i) * block
            window = tables[table, :, pl.ds(pl.multiple_of(down, block), depth)]
            first = pl.multiple_of(first, block)
            pair = jnp.concatenate(
                [ref[pl.ds(first, depth), :], ref[pl.ds(first + block, depth), :]], axis=1
            )
            got = jnp.dot(window, pair, preferred_element_type=jnp.float32).astype(jnp.bfloat16)
            to = jnp.where(table == 0, i, owners - 1 - i)
            results[to, slot, :block, :] = got[:, :LANES]
            results[to, slot, block:, :] = got[:, LANES:]
    for k in range(owners):
        outs[k][...] = results[q ^ k]


def convolve(owners, place, tables, halves, crossing):
    rows = halves[0].shape[1]
    block = rows // 2
    seq = tables.shape[2]
    pair = jax.ShapeDtypeStruct((2, rows, LANES), jnp.bfloat16)
    return pl.pallas_call(
        functools.partial(conv_kernel, owners),
        out_shape=[pair] * owners,
        in_specs=[SMEM] + [VMEM] * (2 * owners + 1),
        out_specs=[VMEM] * owners,
        scratch_shapes=[
            pltpu.VMEM((seq + 2 * block, LANES), jnp.bfloat16),
            pltpu.VMEM((seq // 2 + 2 * block, LANES), jnp.bfloat16),
            pltpu.VMEM((owners, 2, rows, LANES), jnp.bfloat16),
        ],
        compiler_params=params(),
        name="convolve",
    )(place, tables, *halves, *crossing)


def adjoints_kernel(owners, place, key, value, cot, *refs):
    parts = refs[:owners]
    query_adj, key_adj, value_adj = refs[owners:]
    for k in range(owners):
        lanes = pl.ds(pl.multiple_of((place[0] ^ k) * LANES, LANES), LANES)
        mixed, back = parts[k][0], parts[k][1]
        query_adj[:, lanes] = f32_product(cot[:, lanes], mixed).astype(jnp.bfloat16)
        key_adj[:, lanes] = f32_product(back, value[:, lanes]).astype(jnp.bfloat16)
        value_adj[:, lanes] = f32_product(back, key[:, lanes]).astype(jnp.bfloat16)


def adjoints(owners, place, key, value, cot, parts):
    rows, channels = key.shape
    width = channels // owners
    if width == LANES:
        return pl.pallas_call(
            functools.partial(adjoints_kernel, owners),
            out_shape=[jax.ShapeDtypeStruct((rows, channels), jnp.bfloat16)] * 3,
            in_specs=[SMEM] + [VMEM] * (3 + owners),
            out_specs=[VMEM] * 3,
            compiler_params=params(),
            name="adjoints",
        )(place, key, value, cot, *parts)
    both = jnp.zeros((2, rows, channels), jnp.bfloat16)
    for k in range(owners):
        start = (place[0] ^ k) * width
        both = lax.dynamic_update_slice_in_dim(both, parts[k][:, :, :width], start, 2)
    return tuple(
        f32_product(left, right).astype(jnp.bfloat16)
        for left, right in ((cot, both[0]), (both[1], value), (both[1], key))
    )


def on_device(size, ch_size, query, key, value, filters, cot):
    rows, channels = query.shape
    groups, seq = filters.shape
    owners = size // 2
    me = lax.axis_index("ctx")
    place = jnp.stack([me % owners, me // owners]).astype(jnp.int32)
    ch = lax.axis_index("ch")
    group = ch * channels // GW
    sharing = GW // channels

    def swap(array, axis, count, bits):
        return lax.ppermute(array, axis, [(i, i ^ bits) for i in range(count)])

    pairs, singles = split_streams(owners, place, key, value, query, cot)
    halves = [pairs[0]] + [swap(pairs[k], "ctx", size, k) for k in range(1, owners)]
    crossing = [swap(singles[k], "ctx", size, owners ^ k) for k in range(owners)]
    taps = lax.dynamic_index_in_dim(filters, group, 0, keepdims=False)
    tables = toeplitz_tables(taps, rows // 2)
    lags = lag_sums(owners, place, halves, crossing)
    parts = convolve(owners, place, tables, halves, crossing)
    parts = [parts[0]] + [swap(parts[k], "ctx", size, k) for k in range(1, owners)]
    outs = adjoints(owners, place, key, value, cot, parts)

    lags = lags.reshape(size, rows) * (1.0 / math.sqrt(seq * GW))
    bits = 1
    while bits < sharing:
        lags = lags + swap(lags, "ch", ch_size, bits)
        bits *= 2
    span = size // 2
    while span:
        mine = (me // span) % 2
        keep = lax.dynamic_slice_in_dim(lags, mine * span, span, 0)
        give = lax.dynamic_slice_in_dim(lags, (1 - mine) * span, span, 0)
        lags = keep + swap(give, "ctx", size, span)
        span //= 2
    spread = jnp.where(jnp.arange(groups, dtype=jnp.int32)[:, None] == group, lags, 0.0)
    while bits < ch_size:
        spread = spread + swap(spread, "ch", ch_size, bits)
        bits *= 2
    return (*outs, spread)


def solution(mesh):
    return jax.shard_map(
        functools.partial(on_device, mesh.shape["ctx"], mesh.shape["ch"]),
        mesh=mesh,
        in_specs=(P("ctx", "ch"), P("ctx", "ch"), P("ctx", "ch"), P(), P("ctx", "ch")),
        out_specs=(P("ctx", "ch"), P("ctx", "ch"), P("ctx", "ch"), P(None, "ctx")),
        check_vma=False,
    )
```

time: 336 us -> 77.8 us (0.23)
  waiting for transfers between devices: 148 us -> 25.8 us
  blocking collectives: 120 us -> 0 us
  local copies, waits for them, and re-layouts: 28.7 us -> 1.87 us
  starting transfers between devices: 0.08 us -> 25.1 us
  Pallas kernels: 0 us -> 20.3 us
  matrix products: 15.4 us -> 0 us
  between operations: 14.1 us -> 0.74 us
  other arithmetic: 7.32 us -> 3.59 us
    all_gather x2 -> x0, waiting for transfers between devices: 148 us -> none  [the longest x1 77.3 us: on_device(): backward_gathered = lax.all_gather(gated_adj, 'ctx', axis=0, tiled=True)]
    psum x1 -> x0, blocking collectives: 120 us -> none  [on_device(): summed = lax.psum(spread, ('ctx', 'ch'))]
    ppermute x0 -> x15, waiting for transfers between devices: none -> 25.8 us  [swap(): return lax.ppermute(array, axis, [(i, i ^ bits) for i in range(count)])]
    ppermute x0 -> x15, starting transfers between devices: none -> 25.1 us  [swap(): return lax.ppermute(array, axis, [(i, i ^ bits) for i in range(count)])]
    pallas_call x0 -> x5, Pallas kernels: none -> 20.3 us  [the longest x1 6.38 us: convolve(): pl.pallas_call(functools.partial(conv_kernel, owners), out_shape=[pair] *...]
    reshape x10 -> x0, local copies, waits for them, and re-layouts: 17.6 us -> none  [the longest x9 14.7 us: toeplitz_tile(): return repeated.reshape(side_len, 2 * side_len - 1)[:, :side_len]]
    dot_general x10 -> x0, matrix products: 15.4 us -> none  [the longest x8 12.2 us: apply_transpose(): lax.dot_general(band_tile, block_rows, (((0,), (0,)), ((), ())), preferre...]
    cond x21 -> x0, local copies, waits for them, and re-layouts: 7.03 us -> none
  transfers between devices with their start and end apart: 2 -> 15, of which waited for: 2 -> 12; matrix products, arithmetic and copies ran while one was open for 0% -> 3% of each run, Pallas kernels for 0% -> 13%
where the time goes in v1:
time: 77.8 us; the launch traced here: 77.5 us
  waiting for transfers between devices  25.8 us (33%)
  starting transfers between devices  25.1 us (32%)
  Pallas kernels  20.3 us (26%)
  other arithmetic  3.59 us (5%)
  local copies, waits for them, and re-layouts  1.87 us (2%)
    ppermute x15, waiting for transfers between devices, swap(): return lax.ppermute(array, axis, [(i, i ^ bits) for i in range(count)])  25.8 us
    ppermute x15, starting transfers between devices, swap(): return lax.ppermute(array, axis, [(i, i ^ bits) for i in range(count)])  25.1 us
    pallas_call x1, Pallas kernels, convolve(): pl.pallas_call(functools.partial(conv_kernel, owners), out_shape=[pair] *...  6.38 us
    pallas_call x1, Pallas kernels, lag_sums(): pl.pallas_call(functools.partial(lags_kernel, owners), out_shape=jax.Shap...  4.2 us
    pallas_call x1, Pallas kernels, toeplitz_tables(): pl.pallas_call(tables_kernel, out_shape=jax.ShapeDtypeStruct((2, block, s...  3.83 us
    pallas_call x1, Pallas kernels, adjoints(): pl.pallas_call(functools.partial(adjoints_kernel, owners), out_shape=[jax...  3.16 us
    pallas_call x1, Pallas kernels, split_streams(): pl.pallas_call(functools.partial(split_kernel, owners), out_shape=[pair]...  2.77 us
    unnamed x22, local copies, waits for them, and re-layouts  1.59 us
  transfers between devices with their start and end apart: 15, of which 12 were waited for; matrix products, arithmetic and copies ran while one was open for 3% of the time, Pallas kernels for 13%

profile of v1, /device:TPU:0, one launch (start us, length us, event | category | flops | bytes accessed | tf_op | source)
XLA Modules:
  0.0 77.5 jit_solution(7537386593680208810)
XLA Ops:
  1.3 2.8 %split_streams.1 = (bf16[2,512,128]{2,1,0:T(8,128)(2,1)}, bf16[2,512,128]{2,1,0:T(8,128)(2,1)}, bf16[2,512,128]{2,1,0:T(8,128)(2,1)}, bf16[2,512,128]{2,1,0:T(8,...) custom-call(s32[2]{0:T(128)} %pad_add_fusion.place, ...), custom_call_target="tpu_custom_call" | custom-call | tf_op jit(solution)/shard_map/split_streams/pallas_call | solution.py:43
  4.1 4.0 %collective-permute-start.3 = (bf16[512,128]{1,0:T(8,128)(2,1)}, bf16[512,128]{1,0:T(8,128)(2,1)S(1)}, u32[]{:S(2)}, u32[]{:S(2)}) collective-permute-start(bf16[512,128]{1,0:T(8,128)(2,1)} %get-tuple-element.23), channel_id=1, source_target_pairs={{0,16},{4,20},{8,24},{12,28},{16,0},{20,4},{24,8},{28,12},{1,17},{... | collective-permute-start | bytes 393224 | tf_op jit(solution)/shard_map/ppermute | solution.py:271
  8.1 1.3 %collective-permute-start.4 = (bf16[512,128]{1,0:T(8,128)(2,1)}, bf16[512,128]{1,0:T(8,128)(2,1)S(1)}, u32[]{:S(2)}, u32[]{:S(2)}) collective-permute-start(bf16[512,128]{1,0:T(8,128)(2,1)} %get-tuple-element.24), channel_id=1, source_target_pairs={{0,20},{4,16},{8,28},{12,24},{16,4},{20,0},{24,12},{28,8},{1,21},{... | collective-permute-start | bytes 393224 | tf_op jit(solution)/shard_map/ppermute | solution.py:271
  9.6 1.9 %collective-permute-start.1 = (bf16[2,512,128]{2,1,0:T(8,128)(2,1)}, bf16[2,512,128]{2,1,0:T(8,128)(2,1)S(1)}, u32[]{:S(2)}, u32[]{:S(2)}) collective-permute-start(bf16[2,512,128]{2,1,0:T(8,128)(2,1)} %get-tuple-element.21), channel_id=1, source_target_pairs={{0,8},{4,12},{8,0},{12,4},{16,24},{20,28},{24,16},{28,20},{1,9},{5... | collective-permute-start | bytes 786440 | tf_op jit(solution)/shard_map/ppermute | solution.py:271
  11.5 1.4 %collective-permute-start.2 = (bf16[2,512,128]{2,1,0:T(8,128)(2,1)}, bf16[2,512,128]{2,1,0:T(8,128)(2,1)S(1)}, u32[]{:S(2)}, u32[]{:S(2)}) collective-permute-start(bf16[2,512,128]{2,1,0:T(8,128)(2,1)} %get-tuple-element.22), channel_id=1, source_target_pairs={{0,12},{4,8},{8,4},{12,0},{16,28},{20,24},{24,20},{28,16},{1,13},{... | collective-permute-start | bytes 786440 | tf_op jit(solution)/shard_map/ppermute | solution.py:271
  12.9 5.4 %collective-permute-done.3.refs_4_ = bf16[512,128]{1,0:T(8,128)(2,1)S(1)} collective-permute-done((bf16[512,128]{1,0:T(8,128)(2,1)}, bf16[512,128]{1,0:T(8,128)(2,1)S(1)}, u32[]{:S(2)}, u32[]{:S(2)}) %collective-permute-start.3) | collective-permute-done | bytes 131104 | tf_op jit(solution)/shard_map/ppermute | solution.py:271
  18.3 2.9 %collective-permute-start.5 = (bf16[512,128]{1,0:T(8,128)(2,1)}, bf16[512,128]{1,0:T(8,128)(2,1)S(1)}, u32[]{:S(2)}, u32[]{:S(2)}) collective-permute-start(bf16[512,128]{1,0:T(8,128)(2,1)} %get-tuple-element.25), channel_id=1, source_target_pairs={{0,24},{4,28},{8,16},{12,20},{16,8},{20,12},{24,0},{28,4},{1,25},{... | collective-permute-start | bytes 393224 | tf_op jit(solution)/shard_map/ppermute | solution.py:271
  21.3 3.6 %collective-permute-start.6 = (bf16[512,128]{1,0:T(8,128)(2,1)}, bf16[512,128]{1,0:T(8,128)(2,1)S(1)}, u32[]{:S(2)}, u32[]{:S(2)}) collective-permute-start(bf16[512,128]{1,0:T(8,128)(2,1)} %get-tuple-element.26), channel_id=1, source_target_pairs={{0,28},{4,24},{8,20},{12,16},{16,12},{20,8},{24,4},{28,0},{1,29},{... | collective-permute-start | bytes 393224 | tf_op jit(solution)/shard_map/ppermute | solution.py:271
  25.7 6.0 %collective-permute-done.5.refs_6_ = bf16[512,128]{1,0:T(8,128)(2,1)S(1)} collective-permute-done((bf16[512,128]{1,0:T(8,128)(2,1)}, bf16[512,128]{1,0:T(8,128)(2,1)S(1)}, u32[]{:S(2)}, u32[]{:S(2)}) %collective-permute-start.5) | collective-permute-done | bytes 131104 | tf_op jit(solution)/shard_map/ppermute | solution.py:271
  31.7 2.0 %collective-permute-done.6.refs_7_ = bf16[512,128]{1,0:T(8,128)(2,1)S(1)} collective-permute-done((bf16[512,128]{1,0:T(8,128)(2,1)}, bf16[512,128]{1,0:T(8,128)(2,1)S(1)}, u32[]{:S(2)}, u32[]{:S(2)}) %collective-permute-start.6) | collective-permute-done | bytes 131104 | tf_op jit(solution)/shard_map/ppermute | solution.py:271
  34.7 4.2 %lag_sums.1 = f32[32,128]{1,0:T(8,128)} custom-call(s32[2]{0:T(128)} %pad_add_fusion.place, bf16[2,512,128]{2,1,0:T(8,128)(2,1)} %get-tuple-element.19.refs_0_, bf16[2,512,128]{2,1,0:T(8,128)(2,1)} %copy-done, bf16[2,512,128]{2,1,0:T(8,128)(2,1)} %copy-done.1, bf16[2,512,128]{2,1,0:T(8,128)(2,1)} %copy-done.2, bf16[512,128]{1,0:T(8,128)(2,1)} %copy-done.3, ...), custom_call_target="tpu_custom_call" | custom-call | tf_op jit(solution)/shard_map/lag_sums/pallas_call | solution.py:151
  40.9 1.9 %collective-permute-start.11 = (f32[4,512]{1,0:T(4,128)S(1)}, f32[4,512]{1,0:T(4,128)S(1)}, u32[]{:S(2)}, u32[]{:S(2)}) collective-permute-start(f32[4,512]{1,0:T(4,128)S(1)} %constant_dynamic-slice_fusion.2), channel_id=1, source_target_pairs={{0,16},{4,20},{8,24},{12,28},{16,0},{20,4},{24,8},{28,12},{1,17},{... | collective-permute-start | bytes 24584 | tf_op jit(solution)/shard_map/ppermute | solution.py:271
  42.9 2.6 %collective-permute-done.11 = f32[4,512]{1,0:T(4,128)S(1)} collective-permute-done((f32[4,512]{1,0:T(4,128)S(1)}, f32[4,512]{1,0:T(4,128)S(1)}, u32[]{:S(2)}, u32[]{:S(2)}) %collective-permute-start.11) | collective-permute-done | bytes 8224 | tf_op jit(solution)/shard_map/ppermute | solution.py:271
  45.5 2.3 %collective-permute-start.12 = (f32[2,512]{1,0:T(2,128)S(1)}, f32[2,512]{1,0:T(2,128)S(1)}, u32[]{:S(2)}, u32[]{:S(2)}) collective-permute-start(f32[2,512]{1,0:T(2,128)S(1)} %constant_dynamic-slice_fusion.1), channel_id=1, source_target_pairs={{0,8},{4,12},{8,0},{12,4},{16,24},{20,28},{24,16},{28,20},{1,9},{5... | collective-permute-start | bytes 12296 | tf_op jit(solution)/shard_map/ppermute | solution.py:271
  48.5 1.0 %collective-permute-done.12 = f32[2,512]{1,0:T(2,128)S(1)} collective-permute-done((f32[2,512]{1,0:T(2,128)S(1)}, f32[2,512]{1,0:T(2,128)S(1)}, u32[]{:S(2)}, u32[]{:S(2)}) %collective-permute-start.12) | collective-permute-done | bytes 4128 | tf_op jit(solution)/shard_map/ppermute | solution.py:271
  50.0 3.8 %toeplitz_tables.1.tables = bf16[2,256,4096]{2,1,0:T(8,128)(2,1)} custom-call(f32[2,4352]{1,0:T(2,128)} %pad_maximum_fusion.rows_ref), custom_call_target="tpu_custom_call" | custom-call | tf_op jit(solution)/shard_map/toeplitz_tables/pallas_call | solution.py:82
  53.9 6.4 %convolve.1 = (bf16[2,512,128]{2,1,0:T(8,128)(2,1)}, bf16[2,512,128]{2,1,0:T(8,128)(2,1)}, bf16[2,512,128]{2,1,0:T(8,128)(2,1)}, bf16[2,512,128]{2,1,0:T(8,128)(2,1)}) custom-call(s32[2]{0:T(128)} %pad_add_fusion.place, bf16[2,256,4096]{2,1,0:T(8,128)(2,1)} %toeplitz_tables.1.tables, bf16[2,512,128]{2,1,0:T(8,128)(2,1)} %get-tuple-element.19.refs_0_, ...), custom_call_target="tpu_custom_call" | custom-call | tf_op jit(solution)/shard_map/convolve/pallas_call | solution.py:212
  60.2 1.5 %collective-permute-start.7 = (bf16[2,512,128]{2,1,0:T(8,128)(2,1)}, bf16[2,512,128]{2,1,0:T(8,128)(2,1)S(1)}, u32[]{:S(2)}, u32[]{:S(2)}) collective-permute-start(bf16[2,512,128]{2,1,0:T(8,128)(2,1)} %get-tuple-element.28), channel_id=1, source_target_pairs={{0,4},{4,0},{8,12},{12,8},{16,20},{20,16},{24,28},{28,24},{1,5},{5... | collective-permute-start | bytes 786440 | tf_op jit(solution)/shard_map/ppermute | solution.py:271
  61.7 2.0 %collective-permute-start.8 = (bf16[2,512,128]{2,1,0:T(8,128)(2,1)}, bf16[2,512,128]{2,1,0:T(8,128)(2,1)S(1)}, u32[]{:S(2)}, u32[]{:S(2)}) collective-permute-start(bf16[2,512,128]{2,1,0:T(8,128)(2,1)} %get-tuple-element.29), channel_id=1, source_target_pairs={{0,8},{4,12},{8,0},{12,4},{16,24},{20,28},{24,16},{28,20},{1,9},{5... | collective-permute-start | bytes 786440 | tf_op jit(solution)/shard_map/ppermute | solution.py:271
  63.9 1.5 %collective-permute-start.14 = (f32[2,512]{1,0:T(2,128)S(1)}, f32[2,512]{1,0:T(2,128)S(1)}, u32[]{:S(2)}, u32[]{:S(2)}) collective-permute-start(f32[2,512]{1,0:T(2,128)S(1)} %broadcast_select_fusion), channel_id=1, source_target_pairs={{0,2},{1,3},{2,0},{3,1},{4,6},{5,7},{6,4},{7,5},{8,10},{9,11},{10,... | collective-permute-start | bytes 12296 | tf_op jit(solution)/shard_map/ppermute | solution.py:271
  65.4 2.1 %collective-permute-done.14 = f32[2,512]{1,0:T(2,128)S(1)} collective-permute-done((f32[2,512]{1,0:T(2,128)S(1)}, f32[2,512]{1,0:T(2,128)S(1)}, u32[]{:S(2)}, u32[]{:S(2)}) %collective-permute-start.14) | collective-permute-done | bytes 4128 | tf_op jit(solution)/shard_map/ppermute | solution.py:271
  68.8 2.0 %collective-permute-done.8.refs_2_ = bf16[2,512,128]{2,1,0:T(8,128)(2,1)S(1)} collective-permute-done((bf16[2,512,128]{2,1,0:T(8,128)(2,1)}, bf16[2,512,128]{2,1,0:T(8,128)(2,1)S(1)}, u32[]{:S(2)}, u32[]{:S(2)}) %collective-permute-start.8) | collective-permute-done | bytes 262176 | tf_op jit(solution)/shard_map/ppermute | solution.py:271
  70.8 2.8 %collective-permute-done.9.refs_3_ = bf16[2,512,128]{2,1,0:T(8,128)(2,1)S(1)} collective-permute-done((bf16[2,512,128]{2,1,0:T(8,128)(2,1)}, bf16[2,512,128]{2,1,0:T(8,128)(2,1)S(1)}, u32[]{:S(2)}, u32[]{:S(2)}) %collective-permute-start.9) | collective-permute-done | bytes 262176 | tf_op jit(solution)/shard_map/ppermute | solution.py:271
  74.3 3.2 %adjoints.1 = (bf16[512,512]{1,0:T(8,128)(2,1)}, bf16[512,512]{1,0:T(8,128)(2,1)}, bf16[512,512]{1,0:T(8,128)(2,1)}) custom-call(s32[2]{0:T(128)} %pad_add_fusion.place, bf16[512,512]{1,0:T(8,128)(2,1)} %key.3, bf16[512,512]{1,0:T(8,128)(2,1)} %value.3, bf16[512,512]{1,0:T(8,128)(2,1)} %cot.3, bf16[2,512,128]{2,1,0:T(8,128)(2,1)} %get-tuple-element.27.refs_0_, ...), custom_call_target="tpu_custom_call" | custom-call | tf_op jit(solution)/shard_map/adjoints/pallas_call | solution.py:242
  (55 shorter events, 8.2 us)
Async XLA Ops:
  4.1 14.2 %collective-permute-start.3 = (bf16[512,128]{1,0:T(8,128)(2,1)}, bf16[512,128]{1,0:T(8,128)(2,1)S(1)}, u32[]{:S(2)}, u32[]{:S(2)}) collective-permute-start(bf16[512,128]{1,0:T(8,128)(2,1)} %get-tuple-element.23), channel_id=1, source_target_pairs={{0,16},{4,20},{8,24},{12,28},{16,0},{20,4},{24,8},{28,12},{1,17},{... | collective-permute-start | bytes 393224 | tf_op jit(solution)/shard_map/ppermute | solution.py:271
  8.1 13.1 %collective-permute-start.4 = (bf16[512,128]{1,0:T(8,128)(2,1)}, bf16[512,128]{1,0:T(8,128)(2,1)S(1)}, u32[]{:S(2)}, u32[]{:S(2)}) collective-permute-start(bf16[512,128]{1,0:T(8,128)(2,1)} %get-tuple-element.24), channel_id=1, source_target_pairs={{0,20},{4,16},{8,28},{12,24},{16,4},{20,0},{24,12},{28,8},{1,21},{... | collective-permute-start | bytes 393224 | tf_op jit(solution)/shard_map/ppermute | solution.py:271
  9.4 24.3 %collective-permute-start = (bf16[2,512,128]{2,1,0:T(8,128)(2,1)}, bf16[2,512,128]{2,1,0:T(8,128)(2,1)S(1)}, u32[]{:S(2)}, u32[]{:S(2)}) collective-permute-start(bf16[2,512,128]{2,1,0:T(8,128)(2,1)} %get-tuple-element.20), channel_id=1, source_target_pairs={{0,4},{4,0},{8,12},{12,8},{16,20},{20,16},{24,28},{28,24},{1,5},{5... | collective-permute-start | bytes 786440 | tf_op jit(solution)/shard_map/ppermute | solution.py:271
  9.6 24.0 %collective-permute-start.1 = (bf16[2,512,128]{2,1,0:T(8,128)(2,1)}, bf16[2,512,128]{2,1,0:T(8,128)(2,1)S(1)}, u32[]{:S(2)}, u32[]{:S(2)}) collective-permute-start(bf16[2,512,128]{2,1,0:T(8,128)(2,1)} %get-tuple-element.21), channel_id=1, source_target_pairs={{0,8},{4,12},{8,0},{12,4},{16,24},{20,28},{24,16},{28,20},{1,9},{5... | collective-permute-start | bytes 786440 | tf_op jit(solution)/shard_map/ppermute | solution.py:271
  11.5 22.5 %collective-permute-start.2 = (bf16[2,512,128]{2,1,0:T(8,128)(2,1)}, bf16[2,512,128]{2,1,0:T(8,128)(2,1)S(1)}, u32[]{:S(2)}, u32[]{:S(2)}) collective-permute-start(bf16[2,512,128]{2,1,0:T(8,128)(2,1)} %get-tuple-element.22), channel_id=1, source_target_pairs={{0,12},{4,8},{8,4},{12,0},{16,28},{20,24},{24,20},{28,16},{1,13},{... | collective-permute-start | bytes 786440 | tf_op jit(solution)/shard_map/ppermute | solution.py:271
  18.3 15.7 %copy-start.3 = (bf16[512,128]{1,0:T(8,128)(2,1)}, bf16[512,128]{1,0:T(8,128)(2,1)S(1)}, u32[]{:S(2)}) copy-start(bf16[512,128]{1,0:T(8,128)(2,1)S(1)} %collective-permute-done.3.refs_4_) | copy-start | bytes 393220
  18.3 13.3 %collective-permute-start.5 = (bf16[512,128]{1,0:T(8,128)(2,1)}, bf16[512,128]{1,0:T(8,128)(2,1)S(1)}, u32[]{:S(2)}, u32[]{:S(2)}) collective-permute-start(bf16[512,128]{1,0:T(8,128)(2,1)} %get-tuple-element.25), channel_id=1, source_target_pairs={{0,24},{4,28},{8,16},{12,20},{16,8},{20,12},{24,0},{28,4},{1,25},{... | collective-permute-start | bytes 393224 | tf_op jit(solution)/shard_map/ppermute | solution.py:271
  21.3 12.8 %copy-start.4 = (bf16[512,128]{1,0:T(8,128)(2,1)}, bf16[512,128]{1,0:T(8,128)(2,1)S(1)}, u32[]{:S(2)}) copy-start(bf16[512,128]{1,0:T(8,128)(2,1)S(1)} %collective-permute-done.4.refs_5_) | copy-start | bytes 393220
  21.3 12.4 %collective-permute-start.6 = (bf16[512,128]{1,0:T(8,128)(2,1)}, bf16[512,128]{1,0:T(8,128)(2,1)S(1)}, u32[]{:S(2)}, u32[]{:S(2)}) collective-permute-start(bf16[512,128]{1,0:T(8,128)(2,1)} %get-tuple-element.26), channel_id=1, source_target_pairs={{0,28},{4,24},{8,20},{12,16},{16,12},{20,8},{24,4},{28,0},{1,29},{... | collective-permute-start | bytes 393224 | tf_op jit(solution)/shard_map/ppermute | solution.py:271
  31.7 2.4 %copy-start.5 = (bf16[512,128]{1,0:T(8,128)(2,1)}, bf16[512,128]{1,0:T(8,128)(2,1)S(1)}, u32[]{:S(2)}) copy-start(bf16[512,128]{1,0:T(8,128)(2,1)S(1)} %collective-permute-done.5.refs_6_) | copy-start | bytes 393220
  33.7 0.7 copy-start
  33.7 0.8 %copy-start.1 = (bf16[2,512,128]{2,1,0:T(8,128)(2,1)}, bf16[2,512,128]{2,1,0:T(8,128)(2,1)S(1)}, u32[]{:S(2)}) copy-start(bf16[2,512,128]{2,1,0:T(8,128)(2,1)S(1)} %collective-permute-done.1.refs_2_) | copy-start | bytes 786436
  34.0 0.7 copy-start.2
  39.7 1.2 %collective-permute-start.10 = (f32[8,512]{1,0:T(8,128)S(1)}, f32[8,512]{1,0:T(8,128)S(1)}, u32[]{:S(2)}, u32[]{:S(2)}) collective-permute-start(f32[8,512]{1,0:T(8,128)S(1)} %mul.27), channel_id=1, source_target_pairs={{0,1},{1,0},{2,3},{3,2},{4,5},{5,4},{6,7},{7,6},{8,9},{9,8},{10,11... | collective-permute-start | bytes 49160 | tf_op jit(solution)/shard_map/ppermute | solution.py:271
  40.9 4.6 %collective-permute-start.11 = (f32[4,512]{1,0:T(4,128)S(1)}, f32[4,512]{1,0:T(4,128)S(1)}, u32[]{:S(2)}, u32[]{:S(2)}) collective-permute-start(f32[4,512]{1,0:T(4,128)S(1)} %constant_dynamic-slice_fusion.2), channel_id=1, source_target_pairs={{0,16},{4,20},{8,24},{12,28},{16,0},{20,4},{24,8},{28,12},{1,17},{... | collective-permute-start | bytes 24584 | tf_op jit(solution)/shard_map/ppermute | solution.py:271
  45.5 3.9 %collective-permute-start.12 = (f32[2,512]{1,0:T(2,128)S(1)}, f32[2,512]{1,0:T(2,128)S(1)}, u32[]{:S(2)}, u32[]{:S(2)}) collective-permute-start(f32[2,512]{1,0:T(2,128)S(1)} %constant_dynamic-slice_fusion.1), channel_id=1, source_target_pairs={{0,8},{4,12},{8,0},{12,4},{16,24},{20,28},{24,16},{28,20},{1,9},{5... | collective-permute-start | bytes 12296 | tf_op jit(solution)/shard_map/ppermute | solution.py:271
  49.4 14.3 %collective-permute-start.13 = (f32[1,512]{1,0:T(1,128)S(1)}, f32[1,512]{1,0:T(1,128)S(1)}, u32[]{:S(2)}, u32[]{:S(2)}) collective-permute-start(f32[1,512]{1,0:T(1,128)S(1)} %constant_dynamic-slice_fusion), channel_id=1, source_target_pairs={{0,4},{4,0},{8,12},{12,8},{16,20},{20,16},{24,28},{28,24},{1,5},{5... | collective-permute-start | bytes 6152 | tf_op jit(solution)/shard_map/ppermute | solution.py:271
  60.2 8.6 %collective-permute-start.7 = (bf16[2,512,128]{2,1,0:T(8,128)(2,1)}, bf16[2,512,128]{2,1,0:T(8,128)(2,1)S(1)}, u32[]{:S(2)}, u32[]{:S(2)}) collective-permute-start(bf16[2,512,128]{2,1,0:T(8,128)(2,1)} %get-tuple-element.28), channel_id=1, source_target_pairs={{0,4},{4,0},{8,12},{12,8},{16,20},{20,16},{24,28},{28,24},{1,5},{5... | collective-permute-start | bytes 786440 | tf_op jit(solution)/shard_map/ppermute | solution.py:271
  61.7 9.1 %collective-permute-start.8 = (bf16[2,512,128]{2,1,0:T(8,128)(2,1)}, bf16[2,512,128]{2,1,0:T(8,128)(2,1)S(1)}, u32[]{:S(2)}, u32[]{:S(2)}) collective-permute-start(bf16[2,512,128]{2,1,0:T(8,128)(2,1)} %get-tuple-element.29), channel_id=1, source_target_pairs={{0,8},{4,12},{8,0},{12,4},{16,24},{20,28},{24,16},{28,20},{1,9},{5... | collective-permute-start | bytes 786440 | tf_op jit(solution)/shard_map/ppermute | solution.py:271
  63.8 9.8 %collective-permute-start.9 = (bf16[2,512,128]{2,1,0:T(8,128)(2,1)}, bf16[2,512,128]{2,1,0:T(8,128)(2,1)S(1)}, u32[]{:S(2)}, u32[]{:S(2)}) collective-permute-start(bf16[2,512,128]{2,1,0:T(8,128)(2,1)} %get-tuple-element.30), channel_id=1, source_target_pairs={{0,12},{4,8},{8,4},{12,0},{16,28},{20,24},{24,20},{28,16},{1,13},{... | collective-permute-start | bytes 786440 | tf_op jit(solution)/shard_map/ppermute | solution.py:271
  63.9 3.6 %collective-permute-start.14 = (f32[2,512]{1,0:T(2,128)S(1)}, f32[2,512]{1,0:T(2,128)S(1)}, u32[]{:S(2)}, u32[]{:S(2)}) collective-permute-start(f32[2,512]{1,0:T(2,128)S(1)} %broadcast_select_fusion), channel_id=1, source_target_pairs={{0,2},{1,3},{2,0},{3,1},{4,6},{5,7},{6,4},{7,5},{8,10},{9,11},{10,... | collective-permute-start | bytes 12296 | tf_op jit(solution)/shard_map/ppermute | solution.py:271
  68.8 4.8 %copy-start.7 = (bf16[2,512,128]{2,1,0:T(8,128)(2,1)}, bf16[2,512,128]{2,1,0:T(8,128)(2,1)S(1)}, u32[]{:S(2)}) copy-start(bf16[2,512,128]{2,1,0:T(8,128)(2,1)S(1)} %collective-permute-done.7.refs_1_) | copy-start | bytes 786436
  70.8 2.8 %copy-start.8 = (bf16[2,512,128]{2,1,0:T(8,128)(2,1)}, bf16[2,512,128]{2,1,0:T(8,128)(2,1)S(1)}, u32[]{:S(2)}) copy-start(bf16[2,512,128]{2,1,0:T(8,128)(2,1)S(1)} %collective-permute-done.8.refs_2_) | copy-start | bytes 786436
  73.6 0.7 copy-start.9
  (1 other events, 0.7 us)

commit v2 on v1

v2 whole, which is shorter than its diff:
```python
import functools
import math

import jax
import jax.numpy as jnp
from jax import lax
from jax.experimental import pallas as pl
from jax.experimental.pallas import tpu as pltpu
from jax.sharding import PartitionSpec as P

GW = 1024
LANES = 128
VMEM_LIMIT = 13 * 1024 * 1024
WHOLE_VMEM = 60 * 1024 * 1024
VMEM = pl.BlockSpec(memory_space=pltpu.VMEM)
ANY = pl.BlockSpec(memory_space=pl.ANY)


def params(limit=VMEM_LIMIT):
    return pltpu.CompilerParams(vmem_limit_bytes=limit)


def whereabouts(owners):
    me = lax.axis_index("ctx")
    return me % owners, me // owners


def f32_product(left, right):
    return left.astype(jnp.float32) * right.astype(jnp.float32)


def cost(flops, moved):
    return pl.CostEstimate(flops=2 * flops, bytes_accessed=moved, transcendentals=0)


def split_kernel(owners, *refs):
    streams, outs, held, sems = refs[:4], refs[4 : 5 + owners], refs[-2], refs[-1]
    q, upper = whereabouts(owners)
    rows = streams[0].shape[0]
    pieces = held.shape[1]
    span = rows // pieces
    copies = []
    for p in range(pieces):
        for i in range(4):
            copy = pltpu.make_async_copy(
                streams[i].at[pl.ds(p * span, span), :], held.at[i, p], sems.at[i, p]
            )
            copy.start()
            copies.append(copy)
    for p in range(pieces):
        for copy in copies[4 * p : 4 * p + 4]:
            copy.wait()
        here = slice(p * span, (p + 1) * span)
        for k in range(owners):
            lanes = pl.ds(pl.multiple_of((q ^ k) * LANES, LANES), LANES)
            key, value, query, cot = (held[i, p, :, lanes] for i in range(4))
            product = f32_product(key, value).astype(jnp.bfloat16)
            gated = f32_product(cot, query).astype(jnp.bfloat16)
            outs[k][0, here, :] = product
            outs[k][1, here, :] = gated
            if k == 0:
                outs[owners][here, :] = jnp.where(upper == 1, gated, product)


def split_streams(owners, key, value, query, cot):
    rows, channels = key.shape
    width = channels // owners
    if width == LANES:
        pair = jax.ShapeDtypeStruct((2, rows, LANES), jnp.bfloat16)
        single = jax.ShapeDtypeStruct((rows, LANES), jnp.bfloat16)
        outs = pl.pallas_call(
            functools.partial(split_kernel, owners),
            out_shape=[pair] * owners + [single],
            in_specs=[ANY] * 4,
            out_specs=[VMEM] * (owners + 1),
            scratch_shapes=[
                pltpu.VMEM((4, 4, rows // 4, channels), jnp.bfloat16),
                pltpu.SemaphoreType.DMA((4, 4)),
            ],
            compiler_params=params(WHOLE_VMEM),
            name="split_streams",
        )(key, value, query, cot)
        return outs[:owners], outs[owners]
    q, upper = whereabouts(owners)
    product = f32_product(key, value).astype(jnp.bfloat16)
    gated = f32_product(cot, query).astype(jnp.bfloat16)
    both = jnp.stack([product, gated]).reshape(2, rows, owners, width)
    both = jnp.pad(both, ((0, 0), (0, 0), (0, 0), (0, LANES - width)))
    pairs = [lax.dynamic_index_in_dim(both, q ^ k, 2, keepdims=False) for k in range(owners)]
    return pairs, jnp.where(upper == 1, pairs[0][1], pairs[0][0])


def fill_table(row, out):
    block, seq = out.shape
    width = row.shape[1]
    sub = lax.broadcasted_iota(jnp.int32, (8, width), 0)
    eight = jnp.broadcast_to(row, (8, width))
    for bit in (1, 2, 4):
        eight = jnp.where((sub & bit) != 0, pltpu.roll(eight, bit, 1), eight)
    for start in range(0, block, 16):
        low = pltpu.roll(eight, start, 1) if start else eight
        high = pltpu.roll(eight, start + 8, 1)
        both = jnp.concatenate([low[:, :seq], high[:, :seq]], axis=0)
        out[start : start + 16, :] = both.astype(jnp.bfloat16)


def table_rows(taps, block):
    zeros = jnp.zeros((block,), jnp.float32)
    taps = taps.astype(jnp.float32)
    down = jnp.concatenate([taps[::-1], zeros])
    down = jnp.concatenate([down[block - 1 :], down[: block - 1]])
    return jnp.stack([down, jnp.concatenate([taps, zeros])])


def tail_rows(rows):
    return -(-2 * rows // (16 * LANES)) * 16


def to_tail(lags, rows):
    high = lax.reduce_precision(lags, 8, 7)
    low = (lags - high).astype(jnp.bfloat16)
    high = high.astype(jnp.bfloat16)
    flat = jnp.concatenate([high.reshape(-1, LANES), low.reshape(-1, LANES)])
    return jnp.pad(flat, ((0, tail_rows(rows) - flat.shape[0]), (0, 0)))


def from_tail(part, rows):
    count = rows // LANES
    pairs = part[rows : rows + 2 * count].astype(jnp.float32)
    return (pairs[:count] + pairs[count:]).reshape(rows)


def fold_diagonals(sums, out):
    blocks, block = sums.shape[0], sums.shape[1]
    steps = block // LANES

    def diagonal(lag):
        total = None
        for a in range(steps):
            b = lag + a
            if b // steps < blocks:
                rows = slice(a * LANES, (a + 1) * LANES)
                cols = slice((b % steps) * LANES, (b % steps + 1) * LANES)
                tile = sums[b // steps, rows, cols]
                total = tile if total is None else total + tile
        return jnp.zeros((LANES, LANES), jnp.float32) if total is None else total

    row = lax.broadcasted_iota(jnp.int32, (LANES, LANES), 0)
    col = lax.broadcasted_iota(jnp.int32, (LANES, LANES), 1)
    sub = lax.broadcasted_iota(jnp.int32, (8, LANES), 0)
    current = diagonal(0)
    for lag in range(out.shape[0]):
        after = diagonal(lag + 1)
        mixed = jnp.where(col >= row, current, after)
        eight = mixed[:8]
        for m in range(1, LANES // 8):
            eight = eight + pltpu.roll(mixed[8 * m : 8 * m + 8], LANES - 8 * m, 1)
        for bit in (1, 2, 4):
            eight = jnp.where((sub & bit) != 0, pltpu.roll(eight, LANES - bit, 1), eight)
        out[lag : lag + 1, :] = jnp.sum(eight, axis=0, keepdims=True)
        current = after


def cross_rows(left, right):
    return lax.dot_general(
        left, right, (((1,), (1,)), ((), ())), preferred_element_type=jnp.float32
    )


def far_lags_kernel(owners, scale, *refs):
    halves, crossing = refs[:owners], refs[owners : 2 * owners]
    out, lane_blocks, sums = refs[2 * owners :]
    q, upper = whereabouts(owners)
    block = halves[0].shape[1] // 2
    half_blocks = 2 * owners
    for k in range(owners):
        for part in range(2):
            rows = slice(part * block, (part + 1) * block)
            lanes = pl.ds(pl.multiple_of((2 * (q ^ k) + part) * LANES, LANES), LANES)
            lane_blocks[upper, :, lanes] = halves[k][upper, rows, :]
            lane_blocks[1 - upper, :, lanes] = crossing[k][rows, :]
    sums[half_blocks * upper] = jnp.zeros((block, block), jnp.float32)
    for i in range(half_blocks):
        count = (half_blocks - i) * LANES
        left = pl.ds(pl.multiple_of((1 - upper) * i * LANES, LANES), count)
        right = pl.ds(pl.multiple_of(upper * i * LANES, LANES), count)
        lag = jnp.where(upper == 1, i, half_blocks - i)
        sums[lag] = cross_rows(lane_blocks[0, :, left], lane_blocks[1, :, right])
    fold_diagonals(sums, out)
    out[...] *= scale


def far_lags(owners, scale, halves, crossing):
    block = halves[0].shape[1] // 2
    half_blocks = 2 * owners
    return pl.pallas_call(
        functools.partial(far_lags_kernel, owners, scale),
        out_shape=jax.ShapeDtypeStruct((half_blocks * block // LANES, LANES), jnp.float32),
        in_specs=[VMEM] * (2 * owners),
        out_specs=VMEM,
        scratch_shapes=[
            pltpu.VMEM((2, block, half_blocks * LANES), jnp.bfloat16),
            pltpu.VMEM((half_blocks + 1, block, block), jnp.float32),
        ],
        compiler_params=params(),
        cost_estimate=cost(1 << 20, 1 << 16),
        name="far_lags",
    )(*halves, *crossing)


def near_kernel(owners, scale, firsts, *refs):
    halves = refs[:owners]
    early = refs[owners : 2 * owners]
    main, near_lags, results, streams, lane_blocks, sums, tables = refs[2 * owners :]
    for which in range(2):
        fill_table(firsts[which : which + 1, :], tables.at[which])
    q, upper = whereabouts(owners)
    rows = halves[0].shape[1]
    block = rows // 2
    half_blocks = 2 * owners
    zeros = jnp.zeros((2, block, LANES), jnp.bfloat16)
    streams[:, :block] = zeros
    streams[:, (half_blocks + 1) * block :] = zeros
    for k in range(owners):
        start = pl.multiple_of(block + (q ^ k) * rows, block)
        streams[:, pl.ds(start, rows), :] = halves[k][...]
        for part in range(2):
            lanes = pl.ds(pl.multiple_of((2 * (q ^ k) + part) * LANES, LANES), LANES)
            lane_blocks[:, :, lanes] = halves[k][:, part * block : (part + 1) * block, :]
    for which in range(2):
        for i in range(owners):
            depth = (2 * i + 2) * block
            if which == 0:
                window = tables[0, :, tables.shape[2] - depth :]
                first, to = 0, i
            else:
                window = tables[1, :, :depth]
                first, to = (half_blocks - 1 - 2 * i) * block, owners - 1 - i
            pair = jnp.concatenate(
                [
                    streams[which, first : first + depth, :],
                    streams[which, first + block : first + block + depth, :],
                ],
                axis=1,
            )
            got = jnp.dot(window, pair, preferred_element_type=jnp.float32)
            results[which, to, :block, :] = got[:, :LANES]
            results[which, to, block:, :] = got[:, LANES:]
    for k in range(owners):
        early[k][...] = results[upper, q ^ k].astype(jnp.bfloat16)
    main[...] = results[1 - upper]
    for lag in range(half_blocks):
        count = (half_blocks - lag) * LANES
        sums[lag] = cross_rows(
            lane_blocks[0, :, :count], lane_blocks[1, :, lag * LANES : lag * LANES + count]
        )
    fold_diagonals(sums, near_lags)
    near_lags[...] *= scale


def near(owners, scale, firsts, halves):
    rows = halves[0].shape[1]
    block = rows // 2
    half_blocks = 2 * owners
    single = jax.ShapeDtypeStruct((rows, LANES), jnp.bfloat16)
    outs = pl.pallas_call(
        functools.partial(near_kernel, owners, scale),
        out_shape=[single] * owners
        + [
            jax.ShapeDtypeStruct((owners, rows, LANES), jnp.float32),
            jax.ShapeDtypeStruct((half_blocks * block // LANES, LANES), jnp.float32),
        ],
        in_specs=[VMEM] * (owners + 1),
        out_specs=[VMEM] * (owners + 2),
        scratch_shapes=[
            pltpu.VMEM((2, owners, rows, LANES), jnp.float32),
            pltpu.VMEM((2, (half_blocks + 2) * block, LANES), jnp.bfloat16),
            pltpu.VMEM((2, block, half_blocks * LANES), jnp.bfloat16),
            pltpu.VMEM((half_blocks, block, block), jnp.float32),
            pltpu.VMEM((2, block, firsts.shape[1] - block), jnp.bfloat16),
        ],
        compiler_params=params(),
        cost_estimate=cost(3 * half_blocks * half_blocks * block * block * LANES, 8 << 20),
        name="near",
    )(firsts, *halves)
    return outs[:owners], outs[owners], outs[owners + 1]


def far_kernel(owners, firsts, main, *refs):
    crossing, outs = refs[:owners], refs[owners : 2 * owners]
    stream, results, table = refs[2 * owners :]
    q, upper = whereabouts(owners)
    rows = crossing[0].shape[0]
    block = rows // 2
    half_blocks = 2 * owners
    zeros = jnp.zeros((block, LANES), jnp.bfloat16)
    stream[:block] = zeros
    stream[(half_blocks + 1) * block :] = zeros
    for k in range(owners):
        start = pl.multiple_of(block + (q ^ k) * rows, block)
        stream[pl.ds(start, rows), :] = crossing[k][...]
    fill_table(firsts[pl.ds(1 - upper, 1), :], table)
    depth = (half_blocks + 1) * block
    for i in range(owners):
        start = jnp.where(upper == 1, half_blocks - 2 - 2 * i, 1 + 2 * i) * block
        window = table[:, pl.ds(pl.multiple_of(start, block), depth)]
        pair = jnp.concatenate([stream[:depth, :], stream[block : block + depth, :]], axis=1)
        got = jnp.dot(window, pair, preferred_element_type=jnp.float32)
        to = jnp.where(upper == 1, i, owners - 1 - i)
        low = main[to, :block, :] + got[:, :LANES]
        high = main[to, block:, :] + got[:, LANES:]
        results[to, :block, :] = low.astype(jnp.bfloat16)
        results[to, block:, :] = high.astype(jnp.bfloat16)
    for k in range(owners):
        outs[k][:rows, :] = results[q ^ k]
        outs[k][rows:, :] = jnp.zeros((tail_rows(rows), LANES), jnp.bfloat16)


def far(owners, firsts, main, crossing):
    rows = crossing[0].shape[0]
    block = rows // 2
    half_blocks = 2 * owners
    pair = jax.ShapeDtypeStruct((rows + tail_rows(rows), LANES), jnp.bfloat16)
    return pl.pallas_call(
        functools.partial(far_kernel, owners),
        out_shape=[pair] * owners,
        in_specs=[VMEM] * (owners + 2),
        out_specs=[VMEM] * owners,
        scratch_shapes=[
            pltpu.VMEM(((half_blocks + 2) * block, LANES), jnp.bfloat16),
            pltpu.VMEM((owners, rows, LANES), jnp.bfloat16),
            pltpu.VMEM((block, firsts.shape[1] - block), jnp.bfloat16),
        ],
        compiler_params=params(),
        cost_estimate=cost(1 << 20, 1 << 16),
        name="far",
    )(firsts, main, *crossing)


def adjoints_kernel(owners, key, value, cot, *refs):
    early, late = refs[:owners], refs[owners : 2 * owners]
    query_adj, key_adj, value_adj = refs[2 * owners :]
    rows = key.shape[0]
    q, upper = whereabouts(owners)
    for k in range(owners):
        lanes = pl.ds(pl.multiple_of((q ^ k) * LANES, LANES), LANES)
        first, second = early[k][...], late[k][:rows, :]
        mixed = jnp.where(upper == 1, second, first)
        back = jnp.where(upper == 1, first, second)
        query_adj[:, lanes] = f32_product(cot[:, lanes], mixed).astype(jnp.bfloat16)
        key_adj[:, lanes] = f32_product(back, value[:, lanes]).astype(jnp.bfloat16)
        value_adj[:, lanes] = f32_product(back, key[:, lanes]).astype(jnp.bfloat16)


def adjoints(owners, key, value, cot, early, late):
    rows, channels = key.shape
    width = channels // owners
    if width == LANES:
        return pl.pallas_call(
            functools.partial(adjoints_kernel, owners),
            out_shape=[jax.ShapeDtypeStruct((rows, channels), jnp.bfloat16)] * 3,
            in_specs=[VMEM] * (3 + 2 * owners),
            out_specs=[VMEM] * 3,
            compiler_params=params(),
            name="adjoints",
        )(key, value, cot, *early, *late)
    q, upper = whereabouts(owners)
    both = jnp.zeros((2, rows, channels), jnp.bfloat16)
    for k in range(owners):
        pair = jnp.stack([early[k][:, :width], late[k][:rows, :width]])
        both = lax.dynamic_update_slice_in_dim(both, pair, (q ^ k) * width, 2)
    mixed = jnp.where(upper == 1, both[1], both[0])
    back = jnp.where(upper == 1, both[0], both[1])
    return tuple(
        f32_product(left, right).astype(jnp.bfloat16)
        for left, right in ((cot, mixed), (back, value), (back, key))
    )


def on_device(size, ch_size, query, key, value, filters, cot):
    rows, channels = query.shape
    groups, seq = filters.shape
    owners = size // 2
    q, upper = whereabouts(owners)
    group = lax.axis_index("ch") * channels // GW
    sharing = GW // channels

    def swap(array, axis, count, bits):
        return lax.ppermute(array, axis, [(i, i ^ bits) for i in range(count)])

    def exchange(parts):
        return [parts[0]] + [swap(parts[k], "ctx", size, k) for k in range(1, owners)]

    pairs, own = split_streams(owners, key, value, query, cot)
    halves = exchange(pairs)
    crossing = [own] + [lax.dynamic_index_in_dim(pair, upper, 0, keepdims=False) for pair in halves[1:]]
    crossing = [swap(stream, "ctx", size, owners) for stream in crossing]
    taps = lax.dynamic_index_in_dim(filters, group, 0, keepdims=False)
    firsts = table_rows(taps, rows // 2)
    scale = 1.0 / math.sqrt(seq * GW)
    early, main, near_lags = near(owners, scale, firsts, halves)
    begun = crossing[: owners // 2]
    begun, early = lax.optimization_barrier((begun, list(early)))
    crossing[: owners // 2] = begun
    early = exchange(early)

    def over_group(lags):
        bits = 1
        while bits < sharing:
            lags = lags + swap(lags, "ch", ch_size, bits)
            bits *= 2
        return lags

    near_lags = over_group(near_lags.reshape(owners, rows))
    come = lax.ppermute(near_lags, "ctx", [(i + owners, i) for i in range(owners)])
    near_lags = jnp.where(upper == 1, 0.0, near_lags + come)
    lags = over_group(far_lags(owners, scale, halves, crossing).reshape(owners, rows)) + near_lags
    parts = far(owners, firsts, main, crossing)
    parts, early[1] = lax.optimization_barrier((list(parts), early[1]))
    filled = [parts[0]]
    for k in range(1, owners):
        tail = to_tail(lax.dynamic_index_in_dim(lags, q ^ k, 0, keepdims=False), rows)
        filled.append(lax.dynamic_update_slice(parts[k], tail, (rows, 0)))
    parts = exchange(filled)
    outs = adjoints(owners, key, value, cot, early, parts)
    mine = lax.dynamic_index_in_dim(lags, q, 0, keepdims=False)
    mine = mine + sum(from_tail(part, rows) for part in parts[1:])
    here = jnp.arange(groups, dtype=jnp.int32)[:, None] == group
    bits = sharing
    spread = jnp.where(here, mine[None, :], 0.0)
    while bits < ch_size:
        spread = spread + swap(spread, "ch", ch_size, bits)
        bits *= 2
    return (*outs, spread)


def solution(mesh):
    return jax.shard_map(
        functools.partial(on_device, mesh.shape["ctx"], mesh.shape["ch"]),
        mesh=mesh,
        in_specs=(P("ctx", "ch"), P("ctx", "ch"), P("ctx", "ch"), P(), P("ctx", "ch")),
        out_specs=(P("ctx", "ch"), P("ctx", "ch"), P("ctx", "ch"), P(None, "ctx")),
        check_vma=False,
    )
```

time: 77.8 us -> 58.8 us (0.76)
  Pallas kernels: 20.3 us -> 12.3 us
  starting transfers between devices: 25.1 us -> 20.3 us
  waiting for transfers between devices: 25.8 us -> 22.2 us
  other arithmetic: 3.59 us -> 0.98 us
    pallas_call x3, Pallas kernels: 14.4 us -> 7.91 us  [the longest x1 3.63 us: near(): pl.pallas_call(functools.partial(near_kernel, owners, scale), out_shape=[...]
    ppermute x15 -> x16, starting transfers between devices: 25.1 us -> 19 us  [swap(): return lax.ppermute(array, axis, [(i, i ^ bits) for i in range(count)])]
    ppermute x15 -> x16, waiting for transfers between devices: 25.8 us -> 22.2 us  [swap(): return lax.ppermute(array, axis, [(i, i ^ bits) for i in range(count)])]
    pallas_call x1, Pallas kernels: 3.16 us -> 1.62 us  [adjoints(): pl.pallas_call(functools.partial(adjoints_kernel, owners), out_shape=[jax...]
    ppermute x0 -> x1, starting transfers between devices: none -> 1.28 us  [on_device(): lax.ppermute(near_lags, 'ctx', [(i + owners, i) for i in range(owners)])]
    another operation x2 -> x1, other arithmetic: 1.29 us -> 0.04 us  [table_rows(): return jnp.stack([down, jnp.concatenate([taps, zeros])])]
    unnamed x22 -> x12, local copies, waits for them, and re-layouts: 1.59 us -> 0.91 us
  transfers between devices with their start and end apart: 15 -> 17, of which waited for: 12 -> 9; matrix products, arithmetic and copies ran while one was open for 3% -> 3% of each run, Pallas kernels for 13% -> 16%
where the time goes in v2:
time: 58.8 us; the launch traced here: 58.6 us
  waiting for transfers between devices  22.2 us (38%)
  starting transfers between devices  20.3 us (35%)
  Pallas kernels  12.3 us (21%)
  local copies, waits for them, and re-layouts  1.88 us (3%)
  other arithmetic  0.98 us (2%)
  between operations  0.91 us (2%)
    ppermute x16, waiting for transfers between devices, swap(): return lax.ppermute(array, axis, [(i, i ^ bits) for i in range(count)])  22.2 us
    ppermute x16, starting transfers between devices, swap(): return lax.ppermute(array, axis, [(i, i ^ bits) for i in range(count)])  19 us
    pallas_call x1, Pallas kernels, near(): pl.pallas_call(functools.partial(near_kernel, owners, scale), out_shape=[...  3.63 us
    pallas_call x1, Pallas kernels, split_streams(): pl.pallas_call(functools.partial(split_kernel, owners), out_shape=[pair]...  2.77 us
    pallas_call x1, Pallas kernels, far(): pl.pallas_call(functools.partial(far_kernel, owners), out_shape=[pair] *...  2.47 us
    pallas_call x1, Pallas kernels, far_lags(): pl.pallas_call(functools.partial(far_lags_kernel, owners, scale), out_sha...  1.82 us
    pallas_call x1, Pallas kernels, adjoints(): pl.pallas_call(functools.partial(adjoints_kernel, owners), out_shape=[jax...  1.62 us
    ppermute x1, starting transfers between devices, on_device(): lax.ppermute(near_lags, 'ctx', [(i + owners, i) for i in range(owners)])  1.28 us
  transfers between devices with their start and end apart: 17, of which 9 were waited for; matrix products, arithmetic and copies ran while one was open for 3% of the time, Pallas kernels for 16%

profile of v2, /device:TPU:0, one launch (start us, length us, event | category | flops | bytes accessed | tf_op | source)
XLA Modules:
  0.0 58.6 jit_solution(15962503020221621284)
XLA Ops:
  0.6 2.8 %split_streams.1 = (bf16[2,512,128]{2,1,0:T(8,128)(2,1)}, bf16[2,512,128]{2,1,0:T(8,128)(2,1)}, bf16[2,512,128]{2,1,0:T(8,128)(2,1)}, bf16[2,512,128]{2,1,0:T(8,128)(2,1)}, bf16[512,128]{1,0:T(8,128)(2,1)}) custom-call(bf16[512,512]{1,0:T(8,128)(2,1)} %key.1, bf16[512,512]{1,0:T(8,128)(2,1)} %value.1, bf16[512,512]{1,0:T(8,128)(2,1)} %refs_2_.1, ...), custom_call_target="tpu_custom_call" | custom-call | tf_op jit(solution)/shard_map/split_streams/pallas_call | solution.py:71
  3.4 4.1 %collective-permute-start = (bf16[512,128]{1,0:T(8,128)(2,1)}, bf16[512,128]{1,0:T(8,128)(2,1)S(1)}, u32[]{:S(2)}, u32[]{:S(2)}) collective-permute-start(bf16[512,128]{1,0:T(8,128)(2,1)} %get-tuple-element.33), channel_id=1, source_target_pairs={{0,16},{4,20},{8,24},{12,28},{16,0},{20,4},{24,8},{28,12},{1,17},{... | collective-permute-start | bytes 393224 | tf_op jit(solution)/shard_map/ppermute | solution.py:389
  7.5 1.5 %collective-permute-start.1 = (bf16[2,512,128]{2,1,0:T(8,128)(2,1)}, bf16[2,512,128]{2,1,0:T(8,128)(2,1)S(1)}, u32[]{:S(2)}, u32[]{:S(2)}) collective-permute-start(bf16[2,512,128]{2,1,0:T(8,128)(2,1)} %get-tuple-element.34), channel_id=1, source_target_pairs={{0,4},{4,0},{8,12},{12,8},{16,20},{20,16},{24,28},{28,24},{1,5},{5... | collective-permute-start | bytes 786440 | tf_op jit(solution)/shard_map/ppermute | solution.py:389
  9.0 1.6 %collective-permute-start.3 = (bf16[2,512,128]{2,1,0:T(8,128)(2,1)}, bf16[2,512,128]{2,1,0:T(8,128)(2,1)S(1)}, u32[]{:S(2)}, u32[]{:S(2)}) collective-permute-start(bf16[2,512,128]{2,1,0:T(8,128)(2,1)} %get-tuple-element.36), channel_id=1, source_target_pairs={{0,8},{4,12},{8,0},{12,4},{16,24},{20,28},{24,16},{28,20},{1,9},{5... | collective-permute-start | bytes 786440 | tf_op jit(solution)/shard_map/ppermute | solution.py:389
  11.0 0.7 %copy-done.4 = bf16[2,4096]{1,0:T(2,128)(2,1)S(1)} copy-done((bf16[2,4096]{1,0:T(2,128)(2,1)S(1)}, bf16[2,4096]{1,0:T(2,128)(2,1)}, u32[]{:S(2)}) %copy-start.4) | copy-done | bytes 16408
  12.3 3.2 %collective-permute-done.1.refs_1_ = bf16[2,512,128]{2,1,0:T(8,128)(2,1)S(1)} collective-permute-done((bf16[2,512,128]{2,1,0:T(8,128)(2,1)}, bf16[2,512,128]{2,1,0:T(8,128)(2,1)S(1)}, u32[]{:S(2)}, u32[]{:S(2)}) %collective-permute-start.1) | collective-permute-done | bytes 262176 | tf_op jit(solution)/shard_map/ppermute | solution.py:389
  15.9 7.7 %collective-permute-done.3.refs_2_ = bf16[2,512,128]{2,1,0:T(8,128)(2,1)S(1)} collective-permute-done((bf16[2,512,128]{2,1,0:T(8,128)(2,1)}, bf16[2,512,128]{2,1,0:T(8,128)(2,1)S(1)}, u32[]{:S(2)}, u32[]{:S(2)}) %collective-permute-start.3) | collective-permute-done | bytes 262176 | tf_op jit(solution)/shard_map/ppermute | solution.py:389
  23.6 1.4 %collective-permute-start.5 = (bf16[512,128]{1,0:T(8,128)(2,1)S(1)}, bf16[512,128]{1,0:T(8,128)(2,1)S(1)}, u32[]{:S(2)}, u32[]{:S(2)}) collective-permute-start(bf16[512,128]{1,0:T(8,128)(2,1)S(1)} %dynamic-slice_bitcast_fusion.1), channel_id=1, source_target_pairs={{0,16},{4,20},{8,24},{12,28},{16,0},{20,4},{24,8},{28,12},{1,17},{... | collective-permute-start | bytes 393224 | tf_op jit(solution)/shard_map/ppermute | solution.py:389
  25.0 3.2 %collective-permute-done.4.refs_3_ = bf16[2,512,128]{2,1,0:T(8,128)(2,1)S(1)} collective-permute-done((bf16[2,512,128]{2,1,0:T(8,128)(2,1)}, bf16[2,512,128]{2,1,0:T(8,128)(2,1)S(1)}, u32[]{:S(2)}, u32[]{:S(2)}) %collective-permute-start.4) | collective-permute-done | bytes 262176 | tf_op jit(solution)/shard_map/ppermute | solution.py:389
  28.9 0.7 %collective-permute-start.6 = (bf16[512,128]{1,0:T(8,128)(2,1)}, bf16[512,128]{1,0:T(8,128)(2,1)S(1)}, u32[]{:S(2)}, u32[]{:S(2)}) collective-permute-start(bf16[512,128]{1,0:T(8,128)(2,1)} %dynamic-slice_bitcast_fusion), channel_id=1, source_target_pairs={{0,16},{4,20},{8,24},{12,28},{16,0},{20,4},{24,8},{28,12},{1,17},{... | collective-permute-start | bytes 393224 | tf_op jit(solution)/shard_map/ppermute | solution.py:389
  29.6 3.6 %near.1 = (bf16[512,128]{1,0:T(8,128)(2,1)S(1)}, bf16[512,128]{1,0:T(8,128)(2,1)S(1)}, bf16[512,128]{1,0:T(8,128)(2,1)S(1)}, bf16[512,128]{1,0:T(8,128)(2,1)S(1)...) custom-call(f32[2,4352]{1,0:T(2,128)S(1)} %pad_maximum_fusion.firsts, bf16[2,512,128]{2,1,0:T(8,128)(2,1)S(1)} %copy-done.3, ...), custom_call_target="tpu_custom_call" | custom-call | flops 3221225472 | bytes 8388608 | tf_op jit(solution)/shard_map/near/pallas_call | solution.py:266
  33.3 1.2 %collective-permute-done.11 = f32[4,512]{1,0:T(4,128)S(1)} collective-permute-done((f32[4,512]{1,0:T(4,128)S(1)}, f32[4,512]{1,0:T(4,128)S(1)}, u32[]{:S(2)}, u32[]{:S(2)}) %collective-permute-start.11) | collective-permute-done | bytes 8224 | tf_op jit(solution)/shard_map/ppermute | solution.py:389
  34.4 1.3 %collective-permute-start.12 = (f32[4,512]{1,0:T(4,128)S(1)}, f32[4,512]{1,0:T(4,128)S(1)}, u32[]{:S(2)}, u32[]{:S(2)}) collective-permute-start(f32[4,512]{1,0:T(4,128)S(1)} %add.94), channel_id=1, source_target_pairs={{16,0},{20,4},{24,8},{28,12},{17,1},{21,5},{25,9},{29,13},{18,2},{... | collective-permute-start | bytes 24584 | tf_op jit(solution)/shard_map/ppermute | solution.py:415
  35.8 0.8 %collective-permute-done.6.refs_3_.refs_7_ = bf16[512,128]{1,0:T(8,128)(2,1)S(1)} collective-permute-done((bf16[512,128]{1,0:T(8,128)(2,1)}, bf16[512,128]{1,0:T(8,128)(2,1)S(1)}, u32[]{:S(2)}, u32[]{:S(2)}) %collective-permute-start.6) | collective-permute-done | bytes 131104 | tf_op jit(solution)/shard_map/ppermute | solution.py:389
  36.6 1.8 %far_lags.1 = f32[16,128]{1,0:T(8,128)S(1)} custom-call(bf16[2,512,128]{2,1,0:T(8,128)(2,1)S(1)} %copy-done.3, bf16[2,512,128]{2,1,0:T(8,128)(2,1)S(1)} %collective-permute-done.1.refs_1_, bf16[2,512,128]{2,1,0:T(8,128)(2,1)S(1)} %collective-permute-done.3.refs_2_, bf16[2,512,128]{2,1,0:T(8,128)(2,1)S(1)} %collective-permute-done.4.refs_3_, ...), custom_call_target="tpu_custom_call" | custom-call | flops 2097152 | bytes 65536 | tf_op jit(solution)/shard_map/far_lags/pallas_call | solution.py:196
  38.5 1.5 %collective-permute-start.7 = (bf16[512,128]{1,0:T(8,128)(2,1)S(1)}, bf16[512,128]{1,0:T(8,128)(2,1)S(1)}, u32[]{:S(2)}, u32[]{:S(2)}) collective-permute-start(bf16[512,128]{1,0:T(8,128)(2,1)S(1)} %get-tuple-element.50), channel_id=1, source_target_pairs={{0,4},{4,0},{8,12},{12,8},{16,20},{20,16},{24,28},{28,24},{1,5},{5... | collective-permute-start | bytes 393224 | tf_op jit(solution)/shard_map/ppermute | solution.py:389
  40.0 1.7 %collective-permute-start.8 = (bf16[512,128]{1,0:T(8,128)(2,1)S(1)}, bf16[512,128]{1,0:T(8,128)(2,1)S(1)}, u32[]{:S(2)}, u32[]{:S(2)}) collective-permute-start(bf16[512,128]{1,0:T(8,128)(2,1)S(1)} %get-tuple-element.52), channel_id=1, source_target_pairs={{0,8},{4,12},{8,0},{12,4},{16,24},{20,28},{24,16},{28,20},{1,9},{5... | collective-permute-start | bytes 393224 | tf_op jit(solution)/shard_map/ppermute | solution.py:389
  42.1 2.5 %far.1 = (bf16[528,128]{1,0:T(8,128)(2,1)S(1)}, bf16[528,128]{1,0:T(8,128)(2,1)S(1)}, bf16[528,128]{1,0:T(8,128)(2,1)S(1)}, bf16[528,128]{1,0:T(8,128)(2,1)S(1)}) custom-call(f32[2,4352]{1,0:T(2,128)S(1)} %pad_maximum_fusion.firsts, f32[4,512,128]{2,1,0:T(8,128)S(1)} %get-tuple-element.43.main, bf16[512,128]{1,0:T(8,128)(2,1)S(1)} %collective-permute-done.refs_0_.refs_4_, ...), custom_call_target="tpu_custom_call" | custom-call | flops 2097152 | bytes 65536 | tf_op jit(solution)/shard_map/far/pallas_call | solution.py:324
  44.7 2.6 %collective-permute-start.15 = (bf16[528,128]{1,0:T(8,128)(2,1)S(1)}, bf16[528,128]{1,0:T(8,128)(2,1)S(1)}, u32[]{:S(2)}, u32[]{:S(2)}) collective-permute-start(bf16[528,128]{1,0:T(8,128)(2,1)S(1)} %fusion.11), channel_id=1, source_target_pairs={{0,12},{4,8},{8,4},{12,0},{16,28},{20,24},{24,20},{28,16},{1,13},{... | collective-permute-start | bytes 405512 | tf_op jit(solution)/shard_map/ppermute | solution.py:389
  47.7 0.7 %collective-permute-start.13 = (bf16[528,128]{1,0:T(8,128)(2,1)S(1)}, bf16[528,128]{1,0:T(8,128)(2,1)S(1)}, u32[]{:S(2)}, u32[]{:S(2)}) collective-permute-start(bf16[528,128]{1,0:T(8,128)(2,1)S(1)} %fusion.7), channel_id=1, source_target_pairs={{0,4},{4,0},{8,12},{12,8},{16,20},{20,16},{24,28},{28,24},{1,5},{5... | collective-permute-start | bytes 405512 | tf_op jit(solution)/shard_map/ppermute | solution.py:389
  48.4 3.8 %collective-permute-done.15.refs_7_ = bf16[528,128]{1,0:T(8,128)(2,1)S(1)} collective-permute-done((bf16[528,128]{1,0:T(8,128)(2,1)S(1)}, bf16[528,128]{1,0:T(8,128)(2,1)S(1)}, u32[]{:S(2)}, u32[]{:S(2)}) %collective-permute-start.15) | collective-permute-done | bytes 135200 | tf_op jit(solution)/shard_map/ppermute | solution.py:389
  52.2 1.9 %collective-permute-done.14.refs_6_ = bf16[528,128]{1,0:T(8,128)(2,1)S(1)} collective-permute-done((bf16[528,128]{1,0:T(8,128)(2,1)S(1)}, bf16[528,128]{1,0:T(8,128)(2,1)S(1)}, u32[]{:S(2)}, u32[]{:S(2)}) %collective-permute-start.14) | collective-permute-done | bytes 135200 | tf_op jit(solution)/shard_map/ppermute | solution.py:389
  54.3 1.5 %collective-permute-start.16 = (f32[2,512]{1,0:T(2,128)S(1)}, f32[2,512]{1,0:T(2,128)S(1)}, u32[]{:S(2)}, u32[]{:S(2)}) collective-permute-start(f32[2,512]{1,0:T(2,128)S(1)} %broadcast_select_fusion), channel_id=1, source_target_pairs={{0,2},{1,3},{2,0},{3,1},{4,6},{5,7},{6,4},{7,5},{8,10},{9,11},{10,... | collective-permute-start | bytes 12296 | tf_op jit(solution)/shard_map/ppermute | solution.py:389
  55.9 1.6 %adjoints.1 = (bf16[512,512]{1,0:T(8,128)(2,1)}, bf16[512,512]{1,0:T(8,128)(2,1)}, bf16[512,512]{1,0:T(8,128)(2,1)}) custom-call(bf16[512,512]{1,0:T(8,128)(2,1)S(1)} %copy-done, bf16[512,512]{1,0:T(8,128)(2,1)S(1)} %copy-done.1, bf16[512,512]{1,0:T(8,128)(2,1)S(1)} %copy-done.2, bf16[512,128]{1,0:T(8,128)(2,1)S(1)} %get-tuple-element.42.refs_0_, ...), custom_call_target="tpu_custom_call" | custom-call | tf_op jit(solution)/shard_map/adjoints/pallas_call | solution.py:359
  (58 shorter events, 4.4 us)
Async XLA Ops:
  3.4 32.3 %collective-permute-start = (bf16[512,128]{1,0:T(8,128)(2,1)}, bf16[512,128]{1,0:T(8,128)(2,1)S(1)}, u32[]{:S(2)}, u32[]{:S(2)}) collective-permute-start(bf16[512,128]{1,0:T(8,128)(2,1)} %get-tuple-element.33), channel_id=1, source_target_pairs={{0,16},{4,20},{8,24},{12,28},{16,0},{20,4},{24,8},{28,12},{1,17},{... | collective-permute-start | bytes 393224 | tf_op jit(solution)/shard_map/ppermute | solution.py:389
  7.5 8.0 %collective-permute-start.1 = (bf16[2,512,128]{2,1,0:T(8,128)(2,1)}, bf16[2,512,128]{2,1,0:T(8,128)(2,1)S(1)}, u32[]{:S(2)}, u32[]{:S(2)}) collective-permute-start(bf16[2,512,128]{2,1,0:T(8,128)(2,1)} %get-tuple-element.34), channel_id=1, source_target_pairs={{0,4},{4,0},{8,12},{12,8},{16,20},{20,16},{24,28},{28,24},{1,5},{5... | collective-permute-start | bytes 786440 | tf_op jit(solution)/shard_map/ppermute | solution.py:389
  9.0 14.6 %collective-permute-start.3 = (bf16[2,512,128]{2,1,0:T(8,128)(2,1)}, bf16[2,512,128]{2,1,0:T(8,128)(2,1)S(1)}, u32[]{:S(2)}, u32[]{:S(2)}) collective-permute-start(bf16[2,512,128]{2,1,0:T(8,128)(2,1)} %get-tuple-element.36), channel_id=1, source_target_pairs={{0,8},{4,12},{8,0},{12,4},{16,24},{20,28},{24,16},{28,20},{1,9},{5... | collective-permute-start | bytes 786440 | tf_op jit(solution)/shard_map/ppermute | solution.py:389
  10.6 17.6 %collective-permute-start.4 = (bf16[2,512,128]{2,1,0:T(8,128)(2,1)}, bf16[2,512,128]{2,1,0:T(8,128)(2,1)S(1)}, u32[]{:S(2)}, u32[]{:S(2)}) collective-permute-start(bf16[2,512,128]{2,1,0:T(8,128)(2,1)} %get-tuple-element.37), channel_id=1, source_target_pairs={{0,12},{4,8},{8,4},{12,0},{16,28},{20,24},{24,20},{28,16},{1,13},{... | collective-permute-start | bytes 786440 | tf_op jit(solution)/shard_map/ppermute | solution.py:389
  11.0 0.7 %copy-start.4 = (bf16[2,4096]{1,0:T(2,128)(2,1)S(1)}, bf16[2,4096]{1,0:T(2,128)(2,1)}, u32[]{:S(2)}) copy-start(bf16[2,4096]{1,0:T(2,128)(2,1)} %param.8) | copy-start | bytes 49156
  15.5 14.1 %copy-start.3 = (bf16[2,512,128]{2,1,0:T(8,128)(2,1)S(1)}, bf16[2,512,128]{2,1,0:T(8,128)(2,1)}, u32[]{:S(2)}) copy-start(bf16[2,512,128]{2,1,0:T(8,128)(2,1)} %get-tuple-element.35.refs_0_) | copy-start | bytes 786436
  15.5 20.2 %collective-permute-start.2 = (bf16[512,128]{1,0:T(8,128)(2,1)S(1)}, bf16[512,128]{1,0:T(8,128)(2,1)S(1)}, u32[]{:S(2)}, u32[]{:S(2)}) collective-permute-start(bf16[512,128]{1,0:T(8,128)(2,1)S(1)} %dynamic-slice_bitcast_fusion.2), channel_id=1, source_target_pairs={{0,16},{4,20},{8,24},{12,28},{16,0},{20,4},{24,8},{28,12},{1,17},{... | collective-permute-start | bytes 393224 | tf_op jit(solution)/shard_map/ppermute | solution.py:389
  23.6 12.1 %collective-permute-start.5 = (bf16[512,128]{1,0:T(8,128)(2,1)S(1)}, bf16[512,128]{1,0:T(8,128)(2,1)S(1)}, u32[]{:S(2)}, u32[]{:S(2)}) collective-permute-start(bf16[512,128]{1,0:T(8,128)(2,1)S(1)} %dynamic-slice_bitcast_fusion.1), channel_id=1, source_target_pairs={{0,16},{4,20},{8,24},{12,28},{16,0},{20,4},{24,8},{28,12},{1,17},{... | collective-permute-start | bytes 393224 | tf_op jit(solution)/shard_map/ppermute | solution.py:389
  28.9 7.7 %collective-permute-start.6 = (bf16[512,128]{1,0:T(8,128)(2,1)}, bf16[512,128]{1,0:T(8,128)(2,1)S(1)}, u32[]{:S(2)}, u32[]{:S(2)}) collective-permute-start(bf16[512,128]{1,0:T(8,128)(2,1)} %dynamic-slice_bitcast_fusion), channel_id=1, source_target_pairs={{0,16},{4,20},{8,24},{12,28},{16,0},{20,4},{24,8},{28,12},{1,17},{... | collective-permute-start | bytes 393224 | tf_op jit(solution)/shard_map/ppermute | solution.py:389
  33.2 1.2 %collective-permute-start.11 = (f32[4,512]{1,0:T(4,128)S(1)}, f32[4,512]{1,0:T(4,128)S(1)}, u32[]{:S(2)}, u32[]{:S(2)}) collective-permute-start(f32[4,512]{1,0:T(4,128)S(1)} %reshape.66), channel_id=1, source_target_pairs={{0,1},{1,0},{2,3},{3,2},{4,5},{5,4},{6,7},{7,6},{8,9},{9,8},{10,11... | collective-permute-start | bytes 24584 | tf_op jit(solution)/shard_map/ppermute | solution.py:389
  34.4 10.2 %collective-permute-start.12 = (f32[4,512]{1,0:T(4,128)S(1)}, f32[4,512]{1,0:T(4,128)S(1)}, u32[]{:S(2)}, u32[]{:S(2)}) collective-permute-start(f32[4,512]{1,0:T(4,128)S(1)} %add.94), channel_id=1, source_target_pairs={{16,0},{20,4},{24,8},{28,12},{17,1},{21,5},{25,9},{29,13},{18,2},{... | collective-permute-start | bytes 24584 | tf_op jit(solution)/shard_map/ppermute | solution.py:415
  38.4 6.2 %collective-permute-start.10 = (f32[4,512]{1,0:T(4,128)S(1)}, f32[4,512]{1,0:T(4,128)S(1)}, u32[]{:S(2)}, u32[]{:S(2)}) collective-permute-start(f32[4,512]{1,0:T(4,128)S(1)} %reshape.65), channel_id=1, source_target_pairs={{0,1},{1,0},{2,3},{3,2},{4,5},{5,4},{6,7},{7,6},{8,9},{9,8},{10,11... | collective-permute-start | bytes 24584 | tf_op jit(solution)/shard_map/ppermute | solution.py:389
  38.5 6.2 %collective-permute-start.7 = (bf16[512,128]{1,0:T(8,128)(2,1)S(1)}, bf16[512,128]{1,0:T(8,128)(2,1)S(1)}, u32[]{:S(2)}, u32[]{:S(2)}) collective-permute-start(bf16[512,128]{1,0:T(8,128)(2,1)S(1)} %get-tuple-element.50), channel_id=1, source_target_pairs={{0,4},{4,0},{8,12},{12,8},{16,20},{20,16},{24,28},{28,24},{1,5},{5... | collective-permute-start | bytes 393224 | tf_op jit(solution)/shard_map/ppermute | solution.py:389
  40.0 15.8 %collective-permute-start.8 = (bf16[512,128]{1,0:T(8,128)(2,1)S(1)}, bf16[512,128]{1,0:T(8,128)(2,1)S(1)}, u32[]{:S(2)}, u32[]{:S(2)}) collective-permute-start(bf16[512,128]{1,0:T(8,128)(2,1)S(1)} %get-tuple-element.52), channel_id=1, source_target_pairs={{0,8},{4,12},{8,0},{12,4},{16,24},{20,28},{24,16},{28,20},{1,9},{5... | collective-permute-start | bytes 393224 | tf_op jit(solution)/shard_map/ppermute | solution.py:389
  41.7 14.1 %collective-permute-start.9 = (bf16[512,128]{1,0:T(8,128)(2,1)S(1)}, bf16[512,128]{1,0:T(8,128)(2,1)S(1)}, u32[]{:S(2)}, u32[]{:S(2)}) collective-permute-start(bf16[512,128]{1,0:T(8,128)(2,1)S(1)} %get-tuple-element.53), channel_id=1, source_target_pairs={{0,12},{4,8},{8,4},{12,0},{16,28},{20,24},{24,20},{28,16},{1,13},{... | collective-permute-start | bytes 393224 | tf_op jit(solution)/shard_map/ppermute | solution.py:389
  42.1 13.7 %copy-start = (bf16[512,512]{1,0:T(8,128)(2,1)S(1)}, bf16[512,512]{1,0:T(8,128)(2,1)}, u32[]{:S(2)}) copy-start(bf16[512,512]{1,0:T(8,128)(2,1)} %key.1) | copy-start | bytes 1572868
  42.1 13.7 %copy-start.1 = (bf16[512,512]{1,0:T(8,128)(2,1)S(1)}, bf16[512,512]{1,0:T(8,128)(2,1)}, u32[]{:S(2)}) copy-start(bf16[512,512]{1,0:T(8,128)(2,1)} %value.1) | copy-start | bytes 1572868
  42.1 13.7 %copy-start.2 = (bf16[512,512]{1,0:T(8,128)(2,1)S(1)}, bf16[512,512]{1,0:T(8,128)(2,1)}, u32[]{:S(2)}) copy-start(bf16[512,512]{1,0:T(8,128)(2,1)} %cot.1) | copy-start | bytes 1572868
  44.7 7.5 %collective-permute-start.15 = (bf16[528,128]{1,0:T(8,128)(2,1)S(1)}, bf16[528,128]{1,0:T(8,128)(2,1)S(1)}, u32[]{:S(2)}, u32[]{:S(2)}) collective-permute-start(bf16[528,128]{1,0:T(8,128)(2,1)S(1)} %fusion.11), channel_id=1, source_target_pairs={{0,12},{4,8},{8,4},{12,0},{16,28},{20,24},{24,20},{28,16},{1,13},{... | collective-permute-start | bytes 405512 | tf_op jit(solution)/shard_map/ppermute | solution.py:389
  47.3 6.8 %collective-permute-start.14 = (bf16[528,128]{1,0:T(8,128)(2,1)S(1)}, bf16[528,128]{1,0:T(8,128)(2,1)S(1)}, u32[]{:S(2)}, u32[]{:S(2)}) collective-permute-start(bf16[528,128]{1,0:T(8,128)(2,1)S(1)} %fusion.9), channel_id=1, source_target_pairs={{0,8},{4,12},{8,0},{12,4},{16,24},{20,28},{24,16},{28,20},{1,9},{5... | collective-permute-start | bytes 405512 | tf_op jit(solution)/shard_map/ppermute | solution.py:389
  47.7 6.5 %collective-permute-start.13 = (bf16[528,128]{1,0:T(8,128)(2,1)S(1)}, bf16[528,128]{1,0:T(8,128)(2,1)S(1)}, u32[]{:S(2)}, u32[]{:S(2)}) collective-permute-start(bf16[528,128]{1,0:T(8,128)(2,1)S(1)} %fusion.7), channel_id=1, source_target_pairs={{0,4},{4,0},{8,12},{12,8},{16,20},{20,16},{24,28},{28,24},{1,5},{5... | collective-permute-start | bytes 405512 | tf_op jit(solution)/shard_map/ppermute | solution.py:389
  54.3 3.6 %collective-permute-start.16 = (f32[2,512]{1,0:T(2,128)S(1)}, f32[2,512]{1,0:T(2,128)S(1)}, u32[]{:S(2)}, u32[]{:S(2)}) collective-permute-start(f32[2,512]{1,0:T(2,128)S(1)} %broadcast_select_fusion), channel_id=1, source_target_pairs={{0,2},{1,3},{2,0},{3,1},{4,6},{5,7},{6,4},{7,5},{8,10},{9,11},{10,... | collective-permute-start | bytes 12296 | tf_op jit(solution)/shard_map/ppermute | solution.py:389

commit v3 on v2

--- a/solution.py
+++ b/solution.py
@@ -203,7 +203,7 @@
             pltpu.VMEM((half_blocks + 1, block, block), jnp.float32),
         ],
         compiler_params=params(),
-        cost_estimate=cost(1 << 20, 1 << 16),
+        cost_estimate=cost(half_blocks * half_blocks * block * block * LANES // 2, 2 << 20),
         name="far_lags",
     )(*halves, *crossing)
 
@@ -301,16 +301,23 @@
         stream[pl.ds(start, rows), :] = crossing[k][...]
     fill_table(firsts[pl.ds(1 - upper, 1), :], table)
     depth = (half_blocks + 1) * block
-    for i in range(owners):
-        start = jnp.where(upper == 1, half_blocks - 2 - 2 * i, 1 + 2 * i) * block
-        window = table[:, pl.ds(pl.multiple_of(start, block), depth)]
-        pair = jnp.concatenate([stream[:depth, :], stream[block : block + depth, :]], axis=1)
-        got = jnp.dot(window, pair, preferred_element_type=jnp.float32)
-        to = jnp.where(upper == 1, i, owners - 1 - i)
-        low = main[to, :block, :] + got[:, :LANES]
-        high = main[to, block:, :] + got[:, LANES:]
-        results[to, :block, :] = low.astype(jnp.bfloat16)
-        results[to, block:, :] = high.astype(jnp.bfloat16)
+    pair = jnp.concatenate([stream[:depth, :], stream[block : block + depth, :]], axis=1)
+    for group in range(0, owners, 4):
+        several = range(group, min(group + 4, owners))
+        windows = []
+        for i in several:
+            start = jnp.where(upper == 1, half_blocks - 2 - 2 * i, 1 + 2 * i) * block
+            windows.append(table[:, pl.ds(pl.multiple_of(start, block), depth)])
+        all_got = jnp.dot(
+            jnp.concatenate(windows, axis=0), pair, preferred_element_type=jnp.float32
+        )
+        for n, i in enumerate(several):
+            got = all_got[n * block : (n + 1) * block, :]
+            to = jnp.where(upper == 1, i, owners - 1 - i)
+            low = main[to, :block, :] + got[:, :LANES]
+            high = main[to, block:, :] + got[:, LANES:]
+            results[to, :block, :] = low.astype(jnp.bfloat16)
+            results[to, block:, :] = high.astype(jnp.bfloat16)
     for k in range(owners):
         outs[k][:rows, :] = results[q ^ k]
         outs[k][rows:, :] = jnp.zeros((tail_rows(rows), LANES), jnp.bfloat16)
@@ -331,8 +338,7 @@
             pltpu.VMEM((owners, rows, LANES), jnp.bfloat16),
             pltpu.VMEM((block, firsts.shape[1] - block), jnp.bfloat16),
         ],
-        compiler_params=params(),
-        cost_estimate=cost(1 << 20, 1 << 16),
+        compiler_params=params(VMEM_LIMIT * max(1, owners // 4)),
         name="far",
     )(firsts, main, *crossing)
 
@@ -388,21 +394,21 @@
     def swap(array, axis, count, bits):
         return lax.ppermute(array, axis, [(i, i ^ bits) for i in range(count)])
 
-    def exchange(parts):
-        return [parts[0]] + [swap(parts[k], "ctx", size, k) for k in range(1, owners)]
+    def exchange(parts, order):
+        come = {k: swap(parts[k], "ctx", size, k) for k in order}
+        return [parts[0]] + [come[k] for k in range(1, owners)]
+
+    close, distant = range(1, owners // 2), range(owners // 2, owners)
 
     pairs, own = split_streams(owners, key, value, query, cot)
-    halves = exchange(pairs)
+    halves = exchange(pairs, [*distant, *close])
     crossing = [own] + [lax.dynamic_index_in_dim(pair, upper, 0, keepdims=False) for pair in halves[1:]]
     crossing = [swap(stream, "ctx", size, owners) for stream in crossing]
     taps = lax.dynamic_index_in_dim(filters, group, 0, keepdims=False)
     firsts = table_rows(taps, rows // 2)
     scale = 1.0 / math.sqrt(seq * GW)
     early, main, near_lags = near(owners, scale, firsts, halves)
-    begun = crossing[: owners // 2]
-    begun, early = lax.optimization_barrier((begun, list(early)))
-    crossing[: owners // 2] = begun
-    early = exchange(early)
+    early = exchange(early, [*close, *distant])
 
     def over_group(lags):
         bits = 1
@@ -416,13 +422,13 @@
     near_lags = jnp.where(upper == 1, 0.0, near_lags + come)
     lags = over_group(far_lags(owners, scale, halves, crossing).reshape(owners, rows)) + near_lags
     parts = far(owners, firsts, main, crossing)
-    parts, early[1] = lax.optimization_barrier((list(parts), early[1]))
+    for k in distant:
+        parts, early[k] = lax.optimization_barrier((list(parts), early[k]))
     filled = [parts[0]]
     for k in range(1, owners):
         tail = to_tail(lax.dynamic_index_in_dim(lags, q ^ k, 0, keepdims=False), rows)
         filled.append(lax.dynamic_update_slice(parts[k], tail, (rows, 0)))
-    parts = exchange(filled)
-    outs = adjoints(owners, key, value, cot, early, parts)
+    parts = exchange(filled, [*close, *distant])
     mine = lax.dynamic_index_in_dim(lags, q, 0, keepdims=False)
     mine = mine + sum(from_tail(part, rows) for part in parts[1:])
     here = jnp.arange(groups, dtype=jnp.int32)[:, None] == group
@@ -431,6 +437,7 @@
     while bits < ch_size:
         spread = spread + swap(spread, "ch", ch_size, bits)
         bits *= 2
+    outs = adjoints(owners, key, value, cot, early, parts)
     return (*outs, spread)
 
 

time: 58.8 us -> 57.7 us (0.981)
  waiting for transfers between devices: 22.2 us -> 18 us
  starting transfers between devices: 20.3 us -> 22.3 us
  local copies, waits for them, and re-layouts: 1.88 us -> 3.19 us
    ppermute x16, waiting for transfers between devices: 22.2 us -> 18 us  [swap(): return lax.ppermute(array, axis, [(i, i ^ bits) for i in range(count)])]
    ppermute x16, starting transfers between devices: 19 us -> 21 us  [swap(): return lax.ppermute(array, axis, [(i, i ^ bits) for i in range(count)])]
    squeeze x3, local copies, waits for them, and re-layouts: 0.68 us -> 1.99 us  [on_device(): lax.dynamic_index_in_dim(pair, upper, 0, keepdims=False)]
  transfers between devices with their start and end apart: 17 -> 17, of which waited for: 9 -> 9; matrix products, arithmetic and copies ran while one was open for 3% -> 5% of each run, Pallas kernels for 16% -> 16%
where the time goes in v3:
time: 57.7 us; the launch traced here: 57.4 us
  starting transfers between devices  22.3 us (39%)
  waiting for transfers between devices  18 us (31%)
  Pallas kernels  12 us (21%)
  local copies, waits for them, and re-layouts  3.19 us (6%)
  other arithmetic  0.98 us (2%)
  between operations  0.86 us (1%)
    ppermute x16, starting transfers between devices, swap(): return lax.ppermute(array, axis, [(i, i ^ bits) for i in range(count)])  21 us
    ppermute x16, waiting for transfers between devices, swap(): return lax.ppermute(array, axis, [(i, i ^ bits) for i in range(count)])  18 us
    pallas_call x1, Pallas kernels, near(): pl.pallas_call(functools.partial(near_kernel, owners, scale), out_shape=[...  3.63 us
    pallas_call x1, Pallas kernels, split_streams(): pl.pallas_call(functools.partial(split_kernel, owners), out_shape=[pair]...  2.77 us
    pallas_call x1, Pallas kernels, far(): pl.pallas_call(functools.partial(far_kernel, owners), out_shape=[pair] *...  2.17 us
    squeeze x3, local copies, waits for them, and re-layouts, on_device(): lax.dynamic_index_in_dim(pair, upper, 0, keepdims=False)  1.99 us
    pallas_call x1, Pallas kernels, far_lags(): pl.pallas_call(functools.partial(far_lags_kernel, owners, scale), out_sha...  1.83 us
    pallas_call x1, Pallas kernels, adjoints(): pl.pallas_call(functools.partial(adjoints_kernel, owners), out_shape=[jax...  1.61 us
  transfers between devices with their start and end apart: 17, of which 9 were waited for; matrix products, arithmetic and copies ran while one was open for 5% of the time, Pallas kernels for 16%

profile of v3, /device:TPU:0, one launch (start us, length us, event | category | flops | bytes accessed | tf_op | source)
XLA Modules:
  0.0 57.4 jit_solution(17950923818005405086)
XLA Ops:
  0.6 2.8 %split_streams.1 = (bf16[2,512,128]{2,1,0:T(8,128)(2,1)}, bf16[2,512,128]{2,1,0:T(8,128)(2,1)}, bf16[2,512,128]{2,1,0:T(8,128)(2,1)}, bf16[2,512,128]{2,1,0:T(8,128)(2,1)}, bf16[512,128]{1,0:T(8,128)(2,1)}) custom-call(bf16[512,512]{1,0:T(8,128)(2,1)} %key.1, bf16[512,512]{1,0:T(8,128)(2,1)} %value.1, bf16[512,512]{1,0:T(8,128)(2,1)} %refs_2_.1, ...), custom_call_target="tpu_custom_call" | custom-call | tf_op jit(solution)/shard_map/split_streams/pallas_call | solution.py:71
  3.4 3.0 %collective-permute-start = (bf16[2,512,128]{2,1,0:T(8,128)(2,1)}, bf16[2,512,128]{2,1,0:T(8,128)(2,1)S(1)}, u32[]{:S(2)}, u32[]{:S(2)}) collective-permute-start(bf16[2,512,128]{2,1,0:T(8,128)(2,1)} %get-tuple-element.33), channel_id=1, source_target_pairs={{0,4},{4,0},{8,12},{12,8},{16,20},{20,16},{24,28},{28,24},{1,5},{5... | collective-permute-start | bytes 786440 | tf_op jit(solution)/shard_map/ppermute | solution.py:395
  6.4 1.6 %collective-permute-start.1 = (bf16[2,512,128]{2,1,0:T(8,128)(2,1)}, bf16[2,512,128]{2,1,0:T(8,128)(2,1)S(1)}, u32[]{:S(2)}, u32[]{:S(2)}) collective-permute-start(bf16[2,512,128]{2,1,0:T(8,128)(2,1)} %get-tuple-element.34), channel_id=1, source_target_pairs={{0,8},{4,12},{8,0},{12,4},{16,24},{20,28},{24,16},{28,20},{1,9},{5... | collective-permute-start | bytes 786440 | tf_op jit(solution)/shard_map/ppermute | solution.py:395
  8.0 3.0 %collective-permute-start.4 = (bf16[512,128]{1,0:T(8,128)(2,1)}, bf16[512,128]{1,0:T(8,128)(2,1)S(1)}, u32[]{:S(2)}, u32[]{:S(2)}) collective-permute-start(bf16[512,128]{1,0:T(8,128)(2,1)} %get-tuple-element.39), channel_id=1, source_target_pairs={{0,16},{4,20},{8,24},{12,28},{16,0},{20,4},{24,8},{28,12},{1,17},{... | collective-permute-start | bytes 393224 | tf_op jit(solution)/shard_map/ppermute | solution.py:395
  13.6 3.1 %collective-permute-start.5 = (bf16[512,128]{1,0:T(8,128)(2,1)}, bf16[512,128]{1,0:T(8,128)(2,1)S(1)}, u32[]{:S(2)}, u32[]{:S(2)}) collective-permute-start(bf16[512,128]{1,0:T(8,128)(2,1)} %dynamic-slice_bitcast_fusion.2), channel_id=1, source_target_pairs={{0,16},{4,20},{8,24},{12,28},{16,0},{20,4},{24,8},{28,12},{1,17},{... | collective-permute-start | bytes 393224 | tf_op jit(solution)/shard_map/ppermute | solution.py:395
  16.7 6.2 %collective-permute-done.1.refs_2_ = bf16[2,512,128]{2,1,0:T(8,128)(2,1)S(1)} collective-permute-done((bf16[2,512,128]{2,1,0:T(8,128)(2,1)}, bf16[2,512,128]{2,1,0:T(8,128)(2,1)S(1)}, u32[]{:S(2)}, u32[]{:S(2)}) %collective-permute-start.1) | collective-permute-done | bytes 262176 | tf_op jit(solution)/shard_map/ppermute | solution.py:395
  23.6 3.0 %collective-permute-done.2.refs_3_ = bf16[2,512,128]{2,1,0:T(8,128)(2,1)S(1)} collective-permute-done((bf16[2,512,128]{2,1,0:T(8,128)(2,1)}, bf16[2,512,128]{2,1,0:T(8,128)(2,1)S(1)}, u32[]{:S(2)}, u32[]{:S(2)}) %collective-permute-start.2) | collective-permute-done | bytes 262176 | tf_op jit(solution)/shard_map/ppermute | solution.py:395
  27.3 0.9 %collective-permute-start.7 = (bf16[512,128]{1,0:T(8,128)(2,1)}, bf16[512,128]{1,0:T(8,128)(2,1)S(1)}, u32[]{:S(2)}, u32[]{:S(2)}) collective-permute-start(bf16[512,128]{1,0:T(8,128)(2,1)} %dynamic-slice_bitcast_fusion), channel_id=1, source_target_pairs={{0,16},{4,20},{8,24},{12,28},{16,0},{20,4},{24,8},{28,12},{1,17},{... | collective-permute-start | bytes 393224 | tf_op jit(solution)/shard_map/ppermute | solution.py:395
  28.2 3.6 %near.1 = (bf16[512,128]{1,0:T(8,128)(2,1)S(1)}, bf16[512,128]{1,0:T(8,128)(2,1)S(1)}, bf16[512,128]{1,0:T(8,128)(2,1)S(1)}, bf16[512,128]{1,0:T(8,128)(2,1)S(1)...) custom-call(f32[2,4352]{1,0:T(2,128)S(1)} %pad_maximum_fusion.firsts, bf16[2,512,128]{2,1,0:T(8,128)(2,1)S(1)} %copy-done.3, ...), custom_call_target="tpu_custom_call" | custom-call | flops 3221225472 | bytes 8388608 | tf_op jit(solution)/shard_map/near/pallas_call | solution.py:266
  31.9 1.2 %collective-permute-done.11 = f32[4,512]{1,0:T(4,128)S(1)} collective-permute-done((f32[4,512]{1,0:T(4,128)S(1)}, f32[4,512]{1,0:T(4,128)S(1)}, u32[]{:S(2)}, u32[]{:S(2)}) %collective-permute-start.11) | collective-permute-done | bytes 8224 | tf_op jit(solution)/shard_map/ppermute | solution.py:395
  33.1 1.8 %collective-permute-start.8 = (bf16[512,128]{1,0:T(8,128)(2,1)S(1)}, bf16[512,128]{1,0:T(8,128)(2,1)S(1)}, u32[]{:S(2)}, u32[]{:S(2)}) collective-permute-start(bf16[512,128]{1,0:T(8,128)(2,1)S(1)} %get-tuple-element.44), channel_id=1, source_target_pairs={{0,8},{4,12},{8,0},{12,4},{16,24},{20,28},{24,16},{28,20},{1,9},{5... | collective-permute-start | bytes 393224 | tf_op jit(solution)/shard_map/ppermute | solution.py:395
  34.9 1.6 %collective-permute-start.9 = (bf16[512,128]{1,0:T(8,128)(2,1)S(1)}, bf16[512,128]{1,0:T(8,128)(2,1)S(1)}, u32[]{:S(2)}, u32[]{:S(2)}) collective-permute-start(bf16[512,128]{1,0:T(8,128)(2,1)S(1)} %get-tuple-element.50), channel_id=1, source_target_pairs={{0,12},{4,8},{8,4},{12,0},{16,28},{20,24},{24,20},{28,16},{1,13},{... | collective-permute-start | bytes 393224 | tf_op jit(solution)/shard_map/ppermute | solution.py:395
  36.4 1.3 %collective-permute-start.12 = (f32[4,512]{1,0:T(4,128)S(1)}, f32[4,512]{1,0:T(4,128)S(1)}, u32[]{:S(2)}, u32[]{:S(2)}) collective-permute-start(f32[4,512]{1,0:T(4,128)S(1)} %add.94), channel_id=1, source_target_pairs={{16,0},{20,4},{24,8},{28,12},{17,1},{21,5},{25,9},{29,13},{18,2},{... | collective-permute-start | bytes 24584 | tf_op jit(solution)/shard_map/ppermute | solution.py:421
  37.7 1.8 %far_lags.1 = f32[16,128]{1,0:T(8,128)S(1)} custom-call(bf16[2,512,128]{2,1,0:T(8,128)(2,1)S(1)} %copy-done.3, bf16[2,512,128]{2,1,0:T(8,128)(2,1)S(1)} %collective-permute-done.refs_1_, bf16[2,512,128]{2,1,0:T(8,128)(2,1)S(1)} %collective-permute-done.1.refs_2_, bf16[2,512,128]{2,1,0:T(8,128)(2,1)S(1)} %collective-permute-done.2.refs_3_, ...), custom_call_target="tpu_custom_call" | custom-call | flops 536870912 | bytes 2097152 | tf_op jit(solution)/shard_map/far_lags/pallas_call | solution.py:196
  39.7 0.7 %collective-permute-start.3 = (bf16[512,128]{1,0:T(8,128)(2,1)S(1)}, bf16[512,128]{1,0:T(8,128)(2,1)S(1)}, u32[]{:S(2)}, u32[]{:S(2)}) collective-permute-start(bf16[512,128]{1,0:T(8,128)(2,1)S(1)} %get-tuple-element.37), channel_id=1, source_target_pairs={{0,4},{4,0},{8,12},{12,8},{16,20},{20,16},{24,28},{28,24},{1,5},{5... | collective-permute-start | bytes 393224 | tf_op jit(solution)/shard_map/ppermute | solution.py:395
  40.4 2.2 %far.1 = (bf16[528,128]{1,0:T(8,128)(2,1)S(1)}, bf16[528,128]{1,0:T(8,128)(2,1)S(1)}, bf16[528,128]{1,0:T(8,128)(2,1)S(1)}, bf16[528,128]{1,0:T(8,128)(2,1)S(1)}) custom-call(f32[2,4352]{1,0:T(2,128)S(1)} %pad_maximum_fusion.firsts, f32[4,512,128]{2,1,0:T(8,128)S(1)} %get-tuple-element.38.main, bf16[512,128]{1,0:T(8,128)(2,1)S(1)} %collective-permute-done.4.refs_0_.refs_4_, ...), custom_call_target="tpu_custom_call" | custom-call | tf_op jit(solution)/shard_map/far/pallas_call | solution.py:331
  42.6 1.0 %collective-permute-done.9.refs_3_ = bf16[512,128]{1,0:T(8,128)(2,1)S(1)} collective-permute-done((bf16[512,128]{1,0:T(8,128)(2,1)S(1)}, bf16[512,128]{1,0:T(8,128)(2,1)S(1)}, u32[]{:S(2)}, u32[]{:S(2)}) %collective-permute-start.9) | collective-permute-done | bytes 131104 | tf_op jit(solution)/shard_map/ppermute | solution.py:395
  43.7 1.9 %collective-permute-start.15 = (bf16[528,128]{1,0:T(8,128)(2,1)S(1)}, bf16[528,128]{1,0:T(8,128)(2,1)S(1)}, u32[]{:S(2)}, u32[]{:S(2)}) collective-permute-start(bf16[528,128]{1,0:T(8,128)(2,1)S(1)} %fusion.11), channel_id=1, source_target_pairs={{0,12},{4,8},{8,4},{12,0},{16,28},{20,24},{24,20},{28,16},{1,13},{... | collective-permute-start | bytes 405512 | tf_op jit(solution)/shard_map/ppermute | solution.py:395
  45.7 0.8 %collective-permute-start.14 = (bf16[528,128]{1,0:T(8,128)(2,1)S(1)}, bf16[528,128]{1,0:T(8,128)(2,1)S(1)}, u32[]{:S(2)}, u32[]{:S(2)}) collective-permute-start(bf16[528,128]{1,0:T(8,128)(2,1)S(1)} %fusion.9), channel_id=1, source_target_pairs={{0,8},{4,12},{8,0},{12,4},{16,24},{20,28},{24,16},{28,20},{1,9},{5... | collective-permute-start | bytes 405512 | tf_op jit(solution)/shard_map/ppermute | solution.py:395
  46.5 0.9 %collective-permute-start.13 = (bf16[528,128]{1,0:T(8,128)(2,1)S(1)}, bf16[528,128]{1,0:T(8,128)(2,1)S(1)}, u32[]{:S(2)}, u32[]{:S(2)}) collective-permute-start(bf16[528,128]{1,0:T(8,128)(2,1)S(1)} %fusion.7), channel_id=1, source_target_pairs={{0,4},{4,0},{8,12},{12,8},{16,20},{20,16},{24,28},{28,24},{1,5},{5... | collective-permute-start | bytes 405512 | tf_op jit(solution)/shard_map/ppermute | solution.py:395
  47.4 3.7 %collective-permute-done.15.refs_7_ = bf16[528,128]{1,0:T(8,128)(2,1)S(1)} collective-permute-done((bf16[528,128]{1,0:T(8,128)(2,1)S(1)}, bf16[528,128]{1,0:T(8,128)(2,1)S(1)}, u32[]{:S(2)}, u32[]{:S(2)}) %collective-permute-start.15) | collective-permute-done | bytes 135200 | tf_op jit(solution)/shard_map/ppermute | solution.py:395
  51.1 1.6 %collective-permute-done.14.refs_6_ = bf16[528,128]{1,0:T(8,128)(2,1)S(1)} collective-permute-done((bf16[528,128]{1,0:T(8,128)(2,1)S(1)}, bf16[528,128]{1,0:T(8,128)(2,1)S(1)}, u32[]{:S(2)}, u32[]{:S(2)}) %collective-permute-start.14) | collective-permute-done | bytes 135200 | tf_op jit(solution)/shard_map/ppermute | solution.py:395
  53.1 1.5 %collective-permute-start.16 = (f32[2,512]{1,0:T(2,128)S(1)}, f32[2,512]{1,0:T(2,128)S(1)}, u32[]{:S(2)}, u32[]{:S(2)}) collective-permute-start(f32[2,512]{1,0:T(2,128)S(1)} %broadcast_select_fusion), channel_id=1, source_target_pairs={{0,2},{1,3},{2,0},{3,1},{4,6},{5,7},{6,4},{7,5},{8,10},{9,11},{10,... | collective-permute-start | bytes 12296 | tf_op jit(solution)/shard_map/ppermute | solution.py:395
  54.6 1.6 %adjoints.1 = (bf16[512,512]{1,0:T(8,128)(2,1)}, bf16[512,512]{1,0:T(8,128)(2,1)}, bf16[512,512]{1,0:T(8,128)(2,1)}) custom-call(bf16[512,512]{1,0:T(8,128)(2,1)S(1)} %copy-done, bf16[512,512]{1,0:T(8,128)(2,1)S(1)} %copy-done.1, bf16[512,512]{1,0:T(8,128)(2,1)S(1)} %copy-done.2, bf16[512,128]{1,0:T(8,128)(2,1)S(1)} %get-tuple-element.36.refs_0_, ...), custom_call_target="tpu_custom_call" | custom-call | tf_op jit(solution)/shard_map/adjoints/pallas_call | solution.py:365
  (58 shorter events, 5.7 us)
Async XLA Ops:
  3.4 9.5 %collective-permute-start = (bf16[2,512,128]{2,1,0:T(8,128)(2,1)}, bf16[2,512,128]{2,1,0:T(8,128)(2,1)S(1)}, u32[]{:S(2)}, u32[]{:S(2)}) collective-permute-start(bf16[2,512,128]{2,1,0:T(8,128)(2,1)} %get-tuple-element.33), channel_id=1, source_target_pairs={{0,4},{4,0},{8,12},{12,8},{16,20},{20,16},{24,28},{28,24},{1,5},{5... | collective-permute-start | bytes 786440 | tf_op jit(solution)/shard_map/ppermute | solution.py:395
  6.4 16.5 %collective-permute-start.1 = (bf16[2,512,128]{2,1,0:T(8,128)(2,1)}, bf16[2,512,128]{2,1,0:T(8,128)(2,1)S(1)}, u32[]{:S(2)}, u32[]{:S(2)}) collective-permute-start(bf16[2,512,128]{2,1,0:T(8,128)(2,1)} %get-tuple-element.34), channel_id=1, source_target_pairs={{0,8},{4,12},{8,0},{12,4},{16,24},{20,28},{24,16},{28,20},{1,9},{5... | collective-permute-start | bytes 786440 | tf_op jit(solution)/shard_map/ppermute | solution.py:395
  8.0 18.6 %collective-permute-start.2 = (bf16[2,512,128]{2,1,0:T(8,128)(2,1)}, bf16[2,512,128]{2,1,0:T(8,128)(2,1)S(1)}, u32[]{:S(2)}, u32[]{:S(2)}) collective-permute-start(bf16[2,512,128]{2,1,0:T(8,128)(2,1)} %get-tuple-element.35), channel_id=1, source_target_pairs={{0,12},{4,8},{8,4},{12,0},{16,28},{20,24},{24,20},{28,16},{1,13},{... | collective-permute-start | bytes 786440 | tf_op jit(solution)/shard_map/ppermute | solution.py:395
  8.0 26.9 %collective-permute-start.4 = (bf16[512,128]{1,0:T(8,128)(2,1)}, bf16[512,128]{1,0:T(8,128)(2,1)S(1)}, u32[]{:S(2)}, u32[]{:S(2)}) collective-permute-start(bf16[512,128]{1,0:T(8,128)(2,1)} %get-tuple-element.39), channel_id=1, source_target_pairs={{0,16},{4,20},{8,24},{12,28},{16,0},{20,4},{24,8},{28,12},{1,17},{... | collective-permute-start | bytes 393224 | tf_op jit(solution)/shard_map/ppermute | solution.py:395
  11.0 0.7 %copy-start.4 = (bf16[2,4096]{1,0:T(2,128)(2,1)S(1)}, bf16[2,4096]{1,0:T(2,128)(2,1)}, u32[]{:S(2)}) copy-start(bf16[2,4096]{1,0:T(2,128)(2,1)} %param.8) | copy-start | bytes 49156
  13.6 14.6 %copy-start.3 = (bf16[2,512,128]{2,1,0:T(8,128)(2,1)S(1)}, bf16[2,512,128]{2,1,0:T(8,128)(2,1)}, u32[]{:S(2)}) copy-start(bf16[2,512,128]{2,1,0:T(8,128)(2,1)} %get-tuple-element.32.refs_0_) | copy-start | bytes 786436
  13.6 22.8 %collective-permute-start.5 = (bf16[512,128]{1,0:T(8,128)(2,1)}, bf16[512,128]{1,0:T(8,128)(2,1)S(1)}, u32[]{:S(2)}, u32[]{:S(2)}) collective-permute-start(bf16[512,128]{1,0:T(8,128)(2,1)} %dynamic-slice_bitcast_fusion.2), channel_id=1, source_target_pairs={{0,16},{4,20},{8,24},{12,28},{16,0},{20,4},{24,8},{28,12},{1,17},{... | collective-permute-start | bytes 393224 | tf_op jit(solution)/shard_map/ppermute | solution.py:395
  23.6 14.1 %collective-permute-start.6 = (bf16[512,128]{1,0:T(8,128)(2,1)}, bf16[512,128]{1,0:T(8,128)(2,1)S(1)}, u32[]{:S(2)}, u32[]{:S(2)}) collective-permute-start(bf16[512,128]{1,0:T(8,128)(2,1)} %dynamic-slice_bitcast_fusion.1), channel_id=1, source_target_pairs={{0,16},{4,20},{8,24},{12,28},{16,0},{20,4},{24,8},{28,12},{1,17},{... | collective-permute-start | bytes 393224 | tf_op jit(solution)/shard_map/ppermute | solution.py:395
  27.3 10.4 %collective-permute-start.7 = (bf16[512,128]{1,0:T(8,128)(2,1)}, bf16[512,128]{1,0:T(8,128)(2,1)S(1)}, u32[]{:S(2)}, u32[]{:S(2)}) collective-permute-start(bf16[512,128]{1,0:T(8,128)(2,1)} %dynamic-slice_bitcast_fusion), channel_id=1, source_target_pairs={{0,16},{4,20},{8,24},{12,28},{16,0},{20,4},{24,8},{28,12},{1,17},{... | collective-permute-start | bytes 393224 | tf_op jit(solution)/shard_map/ppermute | solution.py:395
  31.8 1.2 %collective-permute-start.11 = (f32[4,512]{1,0:T(4,128)S(1)}, f32[4,512]{1,0:T(4,128)S(1)}, u32[]{:S(2)}, u32[]{:S(2)}) collective-permute-start(f32[4,512]{1,0:T(4,128)S(1)} %reshape.66), channel_id=1, source_target_pairs={{0,1},{1,0},{2,3},{3,2},{4,5},{5,4},{6,7},{7,6},{8,9},{9,8},{10,11... | collective-permute-start | bytes 24584 | tf_op jit(solution)/shard_map/ppermute | solution.py:395
  33.1 9.6 %collective-permute-start.8 = (bf16[512,128]{1,0:T(8,128)(2,1)S(1)}, bf16[512,128]{1,0:T(8,128)(2,1)S(1)}, u32[]{:S(2)}, u32[]{:S(2)}) collective-permute-start(bf16[512,128]{1,0:T(8,128)(2,1)S(1)} %get-tuple-element.44), channel_id=1, source_target_pairs={{0,8},{4,12},{8,0},{12,4},{16,24},{20,28},{24,16},{28,20},{1,9},{5... | collective-permute-start | bytes 393224 | tf_op jit(solution)/shard_map/ppermute | solution.py:395
  34.9 8.8 %collective-permute-start.9 = (bf16[512,128]{1,0:T(8,128)(2,1)S(1)}, bf16[512,128]{1,0:T(8,128)(2,1)S(1)}, u32[]{:S(2)}, u32[]{:S(2)}) collective-permute-start(bf16[512,128]{1,0:T(8,128)(2,1)S(1)} %get-tuple-element.50), channel_id=1, source_target_pairs={{0,12},{4,8},{8,4},{12,0},{16,28},{20,24},{24,20},{28,16},{1,13},{... | collective-permute-start | bytes 393224 | tf_op jit(solution)/shard_map/ppermute | solution.py:395
  36.4 7.2 %collective-permute-start.12 = (f32[4,512]{1,0:T(4,128)S(1)}, f32[4,512]{1,0:T(4,128)S(1)}, u32[]{:S(2)}, u32[]{:S(2)}) collective-permute-start(f32[4,512]{1,0:T(4,128)S(1)} %add.94), channel_id=1, source_target_pairs={{16,0},{20,4},{24,8},{28,12},{17,1},{21,5},{25,9},{29,13},{18,2},{... | collective-permute-start | bytes 24584 | tf_op jit(solution)/shard_map/ppermute | solution.py:421
  39.6 4.1 %collective-permute-start.10 = (f32[4,512]{1,0:T(4,128)S(1)}, f32[4,512]{1,0:T(4,128)S(1)}, u32[]{:S(2)}, u32[]{:S(2)}) collective-permute-start(f32[4,512]{1,0:T(4,128)S(1)} %reshape.65), channel_id=1, source_target_pairs={{0,1},{1,0},{2,3},{3,2},{4,5},{5,4},{6,7},{7,6},{8,9},{9,8},{10,11... | collective-permute-start | bytes 24584 | tf_op jit(solution)/shard_map/ppermute | solution.py:395
  39.7 14.9 %collective-permute-start.3 = (bf16[512,128]{1,0:T(8,128)(2,1)S(1)}, bf16[512,128]{1,0:T(8,128)(2,1)S(1)}, u32[]{:S(2)}, u32[]{:S(2)}) collective-permute-start(bf16[512,128]{1,0:T(8,128)(2,1)S(1)} %get-tuple-element.37), channel_id=1, source_target_pairs={{0,4},{4,0},{8,12},{12,8},{16,20},{20,16},{24,28},{28,24},{1,5},{5... | collective-permute-start | bytes 393224 | tf_op jit(solution)/shard_map/ppermute | solution.py:395
  40.4 14.2 %copy-start = (bf16[512,512]{1,0:T(8,128)(2,1)S(1)}, bf16[512,512]{1,0:T(8,128)(2,1)}, u32[]{:S(2)}) copy-start(bf16[512,512]{1,0:T(8,128)(2,1)} %key.1) | copy-start | bytes 1572868
  40.4 14.2 %copy-start.1 = (bf16[512,512]{1,0:T(8,128)(2,1)S(1)}, bf16[512,512]{1,0:T(8,128)(2,1)}, u32[]{:S(2)}) copy-start(bf16[512,512]{1,0:T(8,128)(2,1)} %value.1) | copy-start | bytes 1572868
  40.4 14.2 %copy-start.2 = (bf16[512,512]{1,0:T(8,128)(2,1)S(1)}, bf16[512,512]{1,0:T(8,128)(2,1)}, u32[]{:S(2)}) copy-start(bf16[512,512]{1,0:T(8,128)(2,1)} %cot.1) | copy-start | bytes 1572868
  43.7 7.4 %collective-permute-start.15 = (bf16[528,128]{1,0:T(8,128)(2,1)S(1)}, bf16[528,128]{1,0:T(8,128)(2,1)S(1)}, u32[]{:S(2)}, u32[]{:S(2)}) collective-permute-start(bf16[528,128]{1,0:T(8,128)(2,1)S(1)} %fusion.11), channel_id=1, source_target_pairs={{0,12},{4,8},{8,4},{12,0},{16,28},{20,24},{24,20},{28,16},{1,13},{... | collective-permute-start | bytes 405512 | tf_op jit(solution)/shard_map/ppermute | solution.py:395
  45.7 7.1 %collective-permute-start.14 = (bf16[528,128]{1,0:T(8,128)(2,1)S(1)}, bf16[528,128]{1,0:T(8,128)(2,1)S(1)}, u32[]{:S(2)}, u32[]{:S(2)}) collective-permute-start(bf16[528,128]{1,0:T(8,128)(2,1)S(1)} %fusion.9), channel_id=1, source_target_pairs={{0,8},{4,12},{8,0},{12,4},{16,24},{20,28},{24,16},{28,20},{1,9},{5... | collective-permute-start | bytes 405512 | tf_op jit(solution)/shard_map/ppermute | solution.py:395
  46.5 6.5 %collective-permute-start.13 = (bf16[528,128]{1,0:T(8,128)(2,1)S(1)}, bf16[528,128]{1,0:T(8,128)(2,1)S(1)}, u32[]{:S(2)}, u32[]{:S(2)}) collective-permute-start(bf16[528,128]{1,0:T(8,128)(2,1)S(1)} %fusion.7), channel_id=1, source_target_pairs={{0,4},{4,0},{8,12},{12,8},{16,20},{20,16},{24,28},{28,24},{1,5},{5... | collective-permute-start | bytes 405512 | tf_op jit(solution)/shard_map/ppermute | solution.py:395
  53.1 3.6 %collective-permute-start.16 = (f32[2,512]{1,0:T(2,128)S(1)}, f32[2,512]{1,0:T(2,128)S(1)}, u32[]{:S(2)}, u32[]{:S(2)}) collective-permute-start(f32[2,512]{1,0:T(2,128)S(1)} %broadcast_select_fusion), channel_id=1, source_target_pairs={{0,2},{1,3},{2,0},{3,1},{4,6},{5,7},{6,4},{7,5},{8,10},{9,11},{10,... | collective-permute-start | bytes 12296 | tf_op jit(solution)/shard_map/ppermute | solution.py:395

commit v4 on v3

--- a/solution.py
+++ b/solution.py
@@ -417,12 +417,12 @@
             bits *= 2
         return lags
 
-    near_lags = over_group(near_lags.reshape(owners, rows))
+    near_lags = near_lags.reshape(owners, rows)
     come = lax.ppermute(near_lags, "ctx", [(i + owners, i) for i in range(owners)])
     near_lags = jnp.where(upper == 1, 0.0, near_lags + come)
-    lags = over_group(far_lags(owners, scale, halves, crossing).reshape(owners, rows)) + near_lags
+    lags = over_group(far_lags(owners, scale, halves, crossing).reshape(owners, rows) + near_lags)
     parts = far(owners, firsts, main, crossing)
-    for k in distant:
+    for k in reversed(distant):
         parts, early[k] = lax.optimization_barrier((list(parts), early[k]))
     filled = [parts[0]]
     for k in range(1, owners):

time: 57.7 us -> 57.4 us (level)
  starting transfers between devices: 22.3 us -> 23.2 us
  local copies, waits for them, and re-layouts: 3.19 us -> 2.54 us
    ppermute x16 -> x15, starting transfers between devices: 21 us -> 22 us  [swap(): return lax.ppermute(array, axis, [(i, i ^ bits) for i in range(count)])]
    squeeze x3, local copies, waits for them, and re-layouts: 1.99 us -> 1.34 us  [on_device(): lax.dynamic_index_in_dim(pair, upper, 0, keepdims=False)]
    ppermute x16 -> x15, waiting for transfers between devices: 18 us -> 17.5 us  [swap(): return lax.ppermute(array, axis, [(i, i ^ bits) for i in range(count)])]
  transfers between devices with their start and end apart: 17 -> 16, of which waited for: 9 -> 9; matrix products, arithmetic and copies ran while one was open for 5% -> 4% of each run, Pallas kernels for 16% -> 16%
where the time goes in v4:
time: 57.4 us; the launch traced here: 57.1 us
  starting transfers between devices  23.2 us (40%)
  waiting for transfers between devices  17.5 us (30%)
  Pallas kernels  12 us (21%)
  local copies, waits for them, and re-layouts  2.54 us (4%)
  other arithmetic  0.99 us (2%)
  between operations  0.87 us (2%)
    ppermute x15, starting transfers between devices, swap(): return lax.ppermute(array, axis, [(i, i ^ bits) for i in range(count)])  22 us
    ppermute x15, waiting for transfers between devices, swap(): return lax.ppermute(array, axis, [(i, i ^ bits) for i in range(count)])  17.5 us
    pallas_call x1, Pallas kernels, near(): pl.pallas_call(functools.partial(near_kernel, owners, scale), out_shape=[...  3.62 us
    pallas_call x1, Pallas kernels, split_streams(): pl.pallas_call(functools.partial(split_kernel, owners), out_shape=[pair]...  2.77 us
    pallas_call x1, Pallas kernels, far(): pl.pallas_call(functools.partial(far_kernel, owners), out_shape=[pair] *...  2.17 us
    pallas_call x1, Pallas kernels, far_lags(): pl.pallas_call(functools.partial(far_lags_kernel, owners, scale), out_sha...  1.82 us
    pallas_call x1, Pallas kernels, adjoints(): pl.pallas_call(functools.partial(adjoints_kernel, owners), out_shape=[jax...  1.61 us
    squeeze x3, local copies, waits for them, and re-layouts, on_device(): lax.dynamic_index_in_dim(pair, upper, 0, keepdims=False)  1.34 us
  transfers between devices with their start and end apart: 16, of which 9 were waited for; matrix products, arithmetic and copies ran while one was open for 4% of the time, Pallas kernels for 16%

profile of v4, /device:TPU:0, one launch (start us, length us, event | category | flops | bytes accessed | tf_op | source)
XLA Modules:
  0.0 57.1 jit_solution(14216978983771738284)
XLA Ops:
  0.6 2.8 %split_streams.1 = (bf16[2,512,128]{2,1,0:T(8,128)(2,1)}, bf16[2,512,128]{2,1,0:T(8,128)(2,1)}, bf16[2,512,128]{2,1,0:T(8,128)(2,1)}, bf16[2,512,128]{2,1,0:T(8,128)(2,1)}, bf16[512,128]{1,0:T(8,128)(2,1)}) custom-call(bf16[512,512]{1,0:T(8,128)(2,1)} %key.1, bf16[512,512]{1,0:T(8,128)(2,1)} %value.1, bf16[512,512]{1,0:T(8,128)(2,1)} %refs_2_.1, ...), custom_call_target="tpu_custom_call" | custom-call | tf_op jit(solution)/shard_map/split_streams/pallas_call | solution.py:71
  3.4 3.0 %collective-permute-start = (bf16[2,512,128]{2,1,0:T(8,128)(2,1)}, bf16[2,512,128]{2,1,0:T(8,128)(2,1)S(1)}, u32[]{:S(2)}, u32[]{:S(2)}) collective-permute-start(bf16[2,512,128]{2,1,0:T(8,128)(2,1)} %get-tuple-element.33), channel_id=1, source_target_pairs={{0,4},{4,0},{8,12},{12,8},{16,20},{20,16},{24,28},{28,24},{1,5},{5... | collective-permute-start | bytes 786440 | tf_op jit(solution)/shard_map/ppermute | solution.py:395
  6.4 1.6 %collective-permute-start.1 = (bf16[2,512,128]{2,1,0:T(8,128)(2,1)}, bf16[2,512,128]{2,1,0:T(8,128)(2,1)S(1)}, u32[]{:S(2)}, u32[]{:S(2)}) collective-permute-start(bf16[2,512,128]{2,1,0:T(8,128)(2,1)} %get-tuple-element.34), channel_id=1, source_target_pairs={{0,8},{4,12},{8,0},{12,4},{16,24},{20,28},{24,16},{28,20},{1,9},{5... | collective-permute-start | bytes 786440 | tf_op jit(solution)/shard_map/ppermute | solution.py:395
  8.0 3.0 %collective-permute-start.4 = (bf16[512,128]{1,0:T(8,128)(2,1)}, bf16[512,128]{1,0:T(8,128)(2,1)S(1)}, u32[]{:S(2)}, u32[]{:S(2)}) collective-permute-start(bf16[512,128]{1,0:T(8,128)(2,1)} %get-tuple-element.39), channel_id=1, source_target_pairs={{0,16},{4,20},{8,24},{12,28},{16,0},{20,4},{24,8},{28,12},{1,17},{... | collective-permute-start | bytes 393224 | tf_op jit(solution)/shard_map/ppermute | solution.py:395
  11.0 0.7 %copy-done.4 = bf16[2,4096]{1,0:T(2,128)(2,1)S(1)} copy-done((bf16[2,4096]{1,0:T(2,128)(2,1)S(1)}, bf16[2,4096]{1,0:T(2,128)(2,1)}, u32[]{:S(2)}) %copy-start.4) | copy-done | bytes 16408
  13.0 3.2 %collective-permute-start.5 = (bf16[512,128]{1,0:T(8,128)(2,1)S(1)}, bf16[512,128]{1,0:T(8,128)(2,1)S(1)}, u32[]{:S(2)}, u32[]{:S(2)}) collective-permute-start(bf16[512,128]{1,0:T(8,128)(2,1)S(1)} %dynamic-slice_bitcast_fusion.2), channel_id=1, source_target_pairs={{0,16},{4,20},{8,24},{12,28},{16,0},{20,4},{24,8},{28,12},{1,17},{... | collective-permute-start | bytes 393224 | tf_op jit(solution)/shard_map/ppermute | solution.py:395
  16.1 6.8 %collective-permute-done.1.refs_2_ = bf16[2,512,128]{2,1,0:T(8,128)(2,1)S(1)} collective-permute-done((bf16[2,512,128]{2,1,0:T(8,128)(2,1)}, bf16[2,512,128]{2,1,0:T(8,128)(2,1)S(1)}, u32[]{:S(2)}, u32[]{:S(2)}) %collective-permute-start.1) | collective-permute-done | bytes 262176 | tf_op jit(solution)/shard_map/ppermute | solution.py:395
  23.6 0.9 %collective-permute-start.6 = (bf16[512,128]{1,0:T(8,128)(2,1)}, bf16[512,128]{1,0:T(8,128)(2,1)S(1)}, u32[]{:S(2)}, u32[]{:S(2)}) collective-permute-start(bf16[512,128]{1,0:T(8,128)(2,1)} %dynamic-slice_bitcast_fusion.1), channel_id=1, source_target_pairs={{0,16},{4,20},{8,24},{12,28},{16,0},{20,4},{24,8},{28,12},{1,17},{... | collective-permute-start | bytes 393224 | tf_op jit(solution)/shard_map/ppermute | solution.py:395
  24.4 2.4 %collective-permute-done.2.refs_3_ = bf16[2,512,128]{2,1,0:T(8,128)(2,1)S(1)} collective-permute-done((bf16[2,512,128]{2,1,0:T(8,128)(2,1)}, bf16[2,512,128]{2,1,0:T(8,128)(2,1)S(1)}, u32[]{:S(2)}, u32[]{:S(2)}) %collective-permute-start.2) | collective-permute-done | bytes 262176 | tf_op jit(solution)/shard_map/ppermute | solution.py:395
  27.5 1.2 %collective-permute-start.7 = (bf16[512,128]{1,0:T(8,128)(2,1)}, bf16[512,128]{1,0:T(8,128)(2,1)S(1)}, u32[]{:S(2)}, u32[]{:S(2)}) collective-permute-start(bf16[512,128]{1,0:T(8,128)(2,1)} %dynamic-slice_bitcast_fusion), channel_id=1, source_target_pairs={{0,16},{4,20},{8,24},{12,28},{16,0},{20,4},{24,8},{28,12},{1,17},{... | collective-permute-start | bytes 393224 | tf_op jit(solution)/shard_map/ppermute | solution.py:395
  28.7 3.6 %near.1 = (bf16[512,128]{1,0:T(8,128)(2,1)S(1)}, bf16[512,128]{1,0:T(8,128)(2,1)S(1)}, bf16[512,128]{1,0:T(8,128)(2,1)S(1)}, bf16[512,128]{1,0:T(8,128)(2,1)S(1)...) custom-call(f32[2,4352]{1,0:T(2,128)S(1)} %pad_maximum_fusion.firsts, bf16[2,512,128]{2,1,0:T(8,128)(2,1)S(1)} %copy-done.3, ...), custom_call_target="tpu_custom_call" | custom-call | flops 3221225472 | bytes 8388608 | tf_op jit(solution)/shard_map/near/pallas_call | solution.py:266
  32.4 1.3 %collective-permute-start.10 = (f32[4,512]{1,0:T(4,128)S(1)}, f32[4,512]{1,0:T(4,128)S(1)}, u32[]{:S(2)}, u32[]{:S(2)}) collective-permute-start(f32[4,512]{1,0:T(4,128)S(1)} %reshape.66), channel_id=1, source_target_pairs={{16,0},{20,4},{24,8},{28,12},{17,1},{21,5},{25,9},{29,13},{18,2},{... | collective-permute-start | bytes 24584 | tf_op jit(solution)/shard_map/ppermute | solution.py:421
  33.7 3.3 %collective-permute-start.8 = (bf16[512,128]{1,0:T(8,128)(2,1)S(1)}, bf16[512,128]{1,0:T(8,128)(2,1)S(1)}, u32[]{:S(2)}, u32[]{:S(2)}) collective-permute-start(bf16[512,128]{1,0:T(8,128)(2,1)S(1)} %get-tuple-element.44), channel_id=1, source_target_pairs={{0,12},{4,8},{8,4},{12,0},{16,28},{20,24},{24,20},{28,16},{1,13},{... | collective-permute-start | bytes 393224 | tf_op jit(solution)/shard_map/ppermute | solution.py:395
  37.0 0.7 %collective-permute-done.7.refs_3_.refs_7_ = bf16[512,128]{1,0:T(8,128)(2,1)S(1)} collective-permute-done((bf16[512,128]{1,0:T(8,128)(2,1)}, bf16[512,128]{1,0:T(8,128)(2,1)S(1)}, u32[]{:S(2)}, u32[]{:S(2)}) %collective-permute-start.7) | collective-permute-done | bytes 131104 | tf_op jit(solution)/shard_map/ppermute | solution.py:395
  37.7 1.8 %far_lags.1 = f32[16,128]{1,0:T(8,128)S(1)} custom-call(bf16[2,512,128]{2,1,0:T(8,128)(2,1)S(1)} %copy-done.3, bf16[2,512,128]{2,1,0:T(8,128)(2,1)S(1)} %collective-permute-done.refs_1_, bf16[2,512,128]{2,1,0:T(8,128)(2,1)S(1)} %collective-permute-done.1.refs_2_, bf16[2,512,128]{2,1,0:T(8,128)(2,1)S(1)} %collective-permute-done.2.refs_3_, ...), custom_call_target="tpu_custom_call" | custom-call | flops 536870912 | bytes 2097152 | tf_op jit(solution)/shard_map/far_lags/pallas_call | solution.py:196
  40.3 2.2 %far.1 = (bf16[528,128]{1,0:T(8,128)(2,1)S(1)}, bf16[528,128]{1,0:T(8,128)(2,1)S(1)}, bf16[528,128]{1,0:T(8,128)(2,1)S(1)}, bf16[528,128]{1,0:T(8,128)(2,1)S(1)}) custom-call(f32[2,4352]{1,0:T(2,128)S(1)} %pad_maximum_fusion.firsts, f32[4,512,128]{2,1,0:T(8,128)S(1)} %get-tuple-element.38.main, bf16[512,128]{1,0:T(8,128)(2,1)S(1)} %collective-permute-done.4.refs_0_.refs_4_, ...), custom_call_target="tpu_custom_call" | custom-call | tf_op jit(solution)/shard_map/far/pallas_call | solution.py:331
  42.5 0.8 %collective-permute-done.9.refs_2_ = bf16[512,128]{1,0:T(8,128)(2,1)S(1)} collective-permute-done((bf16[512,128]{1,0:T(8,128)(2,1)S(1)}, bf16[512,128]{1,0:T(8,128)(2,1)S(1)}, u32[]{:S(2)}, u32[]{:S(2)}) %collective-permute-start.9) | collective-permute-done | bytes 131104 | tf_op jit(solution)/shard_map/ppermute | solution.py:395
  43.4 1.6 %collective-permute-start.14 = (bf16[528,128]{1,0:T(8,128)(2,1)S(1)}, bf16[528,128]{1,0:T(8,128)(2,1)S(1)}, u32[]{:S(2)}, u32[]{:S(2)}) collective-permute-start(bf16[528,128]{1,0:T(8,128)(2,1)S(1)} %fusion.11), channel_id=1, source_target_pairs={{0,12},{4,8},{8,4},{12,0},{16,28},{20,24},{24,20},{28,16},{1,13},{... | collective-permute-start | bytes 405512 | tf_op jit(solution)/shard_map/ppermute | solution.py:395
  45.0 0.8 %collective-permute-start.13 = (bf16[528,128]{1,0:T(8,128)(2,1)S(1)}, bf16[528,128]{1,0:T(8,128)(2,1)S(1)}, u32[]{:S(2)}, u32[]{:S(2)}) collective-permute-start(bf16[528,128]{1,0:T(8,128)(2,1)S(1)} %fusion.9), channel_id=1, source_target_pairs={{0,8},{4,12},{8,0},{12,4},{16,24},{20,28},{24,16},{28,20},{1,9},{5... | collective-permute-start | bytes 405512 | tf_op jit(solution)/shard_map/ppermute | solution.py:395
  45.7 1.3 %collective-permute-start.12 = (bf16[528,128]{1,0:T(8,128)(2,1)S(1)}, bf16[528,128]{1,0:T(8,128)(2,1)S(1)}, u32[]{:S(2)}, u32[]{:S(2)}) collective-permute-start(bf16[528,128]{1,0:T(8,128)(2,1)S(1)} %fusion.7), channel_id=1, source_target_pairs={{0,4},{4,0},{8,12},{12,8},{16,20},{20,16},{24,28},{28,24},{1,5},{5... | collective-permute-start | bytes 405512 | tf_op jit(solution)/shard_map/ppermute | solution.py:395
  47.1 3.7 %collective-permute-done.14.refs_7_ = bf16[528,128]{1,0:T(8,128)(2,1)S(1)} collective-permute-done((bf16[528,128]{1,0:T(8,128)(2,1)S(1)}, bf16[528,128]{1,0:T(8,128)(2,1)S(1)}, u32[]{:S(2)}, u32[]{:S(2)}) %collective-permute-start.14) | collective-permute-done | bytes 135200 | tf_op jit(solution)/shard_map/ppermute | solution.py:395
  50.8 1.3 %collective-permute-done.13.refs_6_ = bf16[528,128]{1,0:T(8,128)(2,1)S(1)} collective-permute-done((bf16[528,128]{1,0:T(8,128)(2,1)S(1)}, bf16[528,128]{1,0:T(8,128)(2,1)S(1)}, u32[]{:S(2)}, u32[]{:S(2)}) %collective-permute-start.13) | collective-permute-done | bytes 135200 | tf_op jit(solution)/shard_map/ppermute | solution.py:395
  52.8 1.5 %collective-permute-start.15 = (f32[2,512]{1,0:T(2,128)S(1)}, f32[2,512]{1,0:T(2,128)S(1)}, u32[]{:S(2)}, u32[]{:S(2)}) collective-permute-start(f32[2,512]{1,0:T(2,128)S(1)} %broadcast_select_fusion), channel_id=1, source_target_pairs={{0,2},{1,3},{2,0},{3,1},{4,6},{5,7},{6,4},{7,5},{8,10},{9,11},{10,... | collective-permute-start | bytes 12296 | tf_op jit(solution)/shard_map/ppermute | solution.py:395
  54.4 1.6 %adjoints.1 = (bf16[512,512]{1,0:T(8,128)(2,1)}, bf16[512,512]{1,0:T(8,128)(2,1)}, bf16[512,512]{1,0:T(8,128)(2,1)}) custom-call(bf16[512,512]{1,0:T(8,128)(2,1)S(1)} %copy-done, bf16[512,512]{1,0:T(8,128)(2,1)S(1)} %copy-done.1, bf16[512,512]{1,0:T(8,128)(2,1)S(1)} %copy-done.2, bf16[512,128]{1,0:T(8,128)(2,1)S(1)} %get-tuple-element.36.refs_0_, ...), custom_call_target="tpu_custom_call" | custom-call | tf_op jit(solution)/shard_map/adjoints/pallas_call | solution.py:365
  (56 shorter events, 5.2 us)
Async XLA Ops:
  3.4 9.5 %collective-permute-start = (bf16[2,512,128]{2,1,0:T(8,128)(2,1)}, bf16[2,512,128]{2,1,0:T(8,128)(2,1)S(1)}, u32[]{:S(2)}, u32[]{:S(2)}) collective-permute-start(bf16[2,512,128]{2,1,0:T(8,128)(2,1)} %get-tuple-element.33), channel_id=1, source_target_pairs={{0,4},{4,0},{8,12},{12,8},{16,20},{20,16},{24,28},{28,24},{1,5},{5... | collective-permute-start | bytes 786440 | tf_op jit(solution)/shard_map/ppermute | solution.py:395
  6.4 16.5 %collective-permute-start.1 = (bf16[2,512,128]{2,1,0:T(8,128)(2,1)}, bf16[2,512,128]{2,1,0:T(8,128)(2,1)S(1)}, u32[]{:S(2)}, u32[]{:S(2)}) collective-permute-start(bf16[2,512,128]{2,1,0:T(8,128)(2,1)} %get-tuple-element.34), channel_id=1, source_target_pairs={{0,8},{4,12},{8,0},{12,4},{16,24},{20,28},{24,16},{28,20},{1,9},{5... | collective-permute-start | bytes 786440 | tf_op jit(solution)/shard_map/ppermute | solution.py:395
  8.0 18.8 %collective-permute-start.2 = (bf16[2,512,128]{2,1,0:T(8,128)(2,1)}, bf16[2,512,128]{2,1,0:T(8,128)(2,1)S(1)}, u32[]{:S(2)}, u32[]{:S(2)}) collective-permute-start(bf16[2,512,128]{2,1,0:T(8,128)(2,1)} %get-tuple-element.35), channel_id=1, source_target_pairs={{0,12},{4,8},{8,4},{12,0},{16,28},{20,24},{24,20},{28,16},{1,13},{... | collective-permute-start | bytes 786440 | tf_op jit(solution)/shard_map/ppermute | solution.py:395
  8.0 25.6 %collective-permute-start.4 = (bf16[512,128]{1,0:T(8,128)(2,1)}, bf16[512,128]{1,0:T(8,128)(2,1)S(1)}, u32[]{:S(2)}, u32[]{:S(2)}) collective-permute-start(bf16[512,128]{1,0:T(8,128)(2,1)} %get-tuple-element.39), channel_id=1, source_target_pairs={{0,16},{4,20},{8,24},{12,28},{16,0},{20,4},{24,8},{28,12},{1,17},{... | collective-permute-start | bytes 393224 | tf_op jit(solution)/shard_map/ppermute | solution.py:395
  11.0 0.7 %copy-start.4 = (bf16[2,4096]{1,0:T(2,128)(2,1)S(1)}, bf16[2,4096]{1,0:T(2,128)(2,1)}, u32[]{:S(2)}) copy-start(bf16[2,4096]{1,0:T(2,128)(2,1)} %param.8) | copy-start | bytes 49156
  13.0 15.8 %copy-start.3 = (bf16[2,512,128]{2,1,0:T(8,128)(2,1)S(1)}, bf16[2,512,128]{2,1,0:T(8,128)(2,1)}, u32[]{:S(2)}) copy-start(bf16[2,512,128]{2,1,0:T(8,128)(2,1)} %get-tuple-element.32.refs_0_) | copy-start | bytes 786436
  13.0 24.0 %collective-permute-start.5 = (bf16[512,128]{1,0:T(8,128)(2,1)S(1)}, bf16[512,128]{1,0:T(8,128)(2,1)S(1)}, u32[]{:S(2)}, u32[]{:S(2)}) collective-permute-start(bf16[512,128]{1,0:T(8,128)(2,1)S(1)} %dynamic-slice_bitcast_fusion.2), channel_id=1, source_target_pairs={{0,16},{4,20},{8,24},{12,28},{16,0},{20,4},{24,8},{28,12},{1,17},{... | collective-permute-start | bytes 393224 | tf_op jit(solution)/shard_map/ppermute | solution.py:395
  23.6 13.5 %collective-permute-start.6 = (bf16[512,128]{1,0:T(8,128)(2,1)}, bf16[512,128]{1,0:T(8,128)(2,1)S(1)}, u32[]{:S(2)}, u32[]{:S(2)}) collective-permute-start(bf16[512,128]{1,0:T(8,128)(2,1)} %dynamic-slice_bitcast_fusion.1), channel_id=1, source_target_pairs={{0,16},{4,20},{8,24},{12,28},{16,0},{20,4},{24,8},{28,12},{1,17},{... | collective-permute-start | bytes 393224 | tf_op jit(solution)/shard_map/ppermute | solution.py:395
  27.5 10.2 %collective-permute-start.7 = (bf16[512,128]{1,0:T(8,128)(2,1)}, bf16[512,128]{1,0:T(8,128)(2,1)S(1)}, u32[]{:S(2)}, u32[]{:S(2)}) collective-permute-start(bf16[512,128]{1,0:T(8,128)(2,1)} %dynamic-slice_bitcast_fusion), channel_id=1, source_target_pairs={{0,16},{4,20},{8,24},{12,28},{16,0},{20,4},{24,8},{28,12},{1,17},{... | collective-permute-start | bytes 393224 | tf_op jit(solution)/shard_map/ppermute | solution.py:395
  32.4 7.2 %collective-permute-start.10 = (f32[4,512]{1,0:T(4,128)S(1)}, f32[4,512]{1,0:T(4,128)S(1)}, u32[]{:S(2)}, u32[]{:S(2)}) collective-permute-start(f32[4,512]{1,0:T(4,128)S(1)} %reshape.66), channel_id=1, source_target_pairs={{16,0},{20,4},{24,8},{28,12},{17,1},{21,5},{25,9},{29,13},{18,2},{... | collective-permute-start | bytes 24584 | tf_op jit(solution)/shard_map/ppermute | solution.py:421
  33.7 8.8 %collective-permute-start.8 = (bf16[512,128]{1,0:T(8,128)(2,1)S(1)}, bf16[512,128]{1,0:T(8,128)(2,1)S(1)}, u32[]{:S(2)}, u32[]{:S(2)}) collective-permute-start(bf16[512,128]{1,0:T(8,128)(2,1)S(1)} %get-tuple-element.44), channel_id=1, source_target_pairs={{0,12},{4,8},{8,4},{12,0},{16,28},{20,24},{24,20},{28,16},{1,13},{... | collective-permute-start | bytes 393224 | tf_op jit(solution)/shard_map/ppermute | solution.py:395
  37.0 6.3 %collective-permute-start.9 = (bf16[512,128]{1,0:T(8,128)(2,1)S(1)}, bf16[512,128]{1,0:T(8,128)(2,1)S(1)}, u32[]{:S(2)}, u32[]{:S(2)}) collective-permute-start(bf16[512,128]{1,0:T(8,128)(2,1)S(1)} %get-tuple-element.49), channel_id=1, source_target_pairs={{0,8},{4,12},{8,0},{12,4},{16,24},{20,28},{24,16},{28,20},{1,9},{5... | collective-permute-start | bytes 393224 | tf_op jit(solution)/shard_map/ppermute | solution.py:395
  39.6 3.7 %collective-permute-start.11 = (f32[4,512]{1,0:T(4,128)S(1)}, f32[4,512]{1,0:T(4,128)S(1)}, u32[]{:S(2)}, u32[]{:S(2)}) collective-permute-start(f32[4,512]{1,0:T(4,128)S(1)} %select_add_fusion), channel_id=1, source_target_pairs={{0,1},{1,0},{2,3},{3,2},{4,5},{5,4},{6,7},{7,6},{8,9},{9,8},{10,11... | collective-permute-start | bytes 24584 | tf_op jit(solution)/shard_map/ppermute | solution.py:395
  39.7 14.6 %collective-permute-start.3 = (bf16[512,128]{1,0:T(8,128)(2,1)S(1)}, bf16[512,128]{1,0:T(8,128)(2,1)S(1)}, u32[]{:S(2)}, u32[]{:S(2)}) collective-permute-start(bf16[512,128]{1,0:T(8,128)(2,1)S(1)} %get-tuple-element.37), channel_id=1, source_target_pairs={{0,4},{4,0},{8,12},{12,8},{16,20},{20,16},{24,28},{28,24},{1,5},{5... | collective-permute-start | bytes 393224 | tf_op jit(solution)/shard_map/ppermute | solution.py:395
  40.3 14.1 %copy-start = (bf16[512,512]{1,0:T(8,128)(2,1)S(1)}, bf16[512,512]{1,0:T(8,128)(2,1)}, u32[]{:S(2)}) copy-start(bf16[512,512]{1,0:T(8,128)(2,1)} %key.1) | copy-start | bytes 1572868
  40.3 14.1 %copy-start.1 = (bf16[512,512]{1,0:T(8,128)(2,1)S(1)}, bf16[512,512]{1,0:T(8,128)(2,1)}, u32[]{:S(2)}) copy-start(bf16[512,512]{1,0:T(8,128)(2,1)} %value.1) | copy-start | bytes 1572868
  40.3 14.1 %copy-start.2 = (bf16[512,512]{1,0:T(8,128)(2,1)S(1)}, bf16[512,512]{1,0:T(8,128)(2,1)}, u32[]{:S(2)}) copy-start(bf16[512,512]{1,0:T(8,128)(2,1)} %cot.1) | copy-start | bytes 1572868
  43.4 7.4 %collective-permute-start.14 = (bf16[528,128]{1,0:T(8,128)(2,1)S(1)}, bf16[528,128]{1,0:T(8,128)(2,1)S(1)}, u32[]{:S(2)}, u32[]{:S(2)}) collective-permute-start(bf16[528,128]{1,0:T(8,128)(2,1)S(1)} %fusion.11), channel_id=1, source_target_pairs={{0,12},{4,8},{8,4},{12,0},{16,28},{20,24},{24,20},{28,16},{1,13},{... | collective-permute-start | bytes 405512 | tf_op jit(solution)/shard_map/ppermute | solution.py:395
  45.0 7.1 %collective-permute-start.13 = (bf16[528,128]{1,0:T(8,128)(2,1)S(1)}, bf16[528,128]{1,0:T(8,128)(2,1)S(1)}, u32[]{:S(2)}, u32[]{:S(2)}) collective-permute-start(bf16[528,128]{1,0:T(8,128)(2,1)S(1)} %fusion.9), channel_id=1, source_target_pairs={{0,8},{4,12},{8,0},{12,4},{16,24},{20,28},{24,16},{28,20},{1,9},{5... | collective-permute-start | bytes 405512 | tf_op jit(solution)/shard_map/ppermute | solution.py:395
  45.7 7.0 %collective-permute-start.12 = (bf16[528,128]{1,0:T(8,128)(2,1)S(1)}, bf16[528,128]{1,0:T(8,128)(2,1)S(1)}, u32[]{:S(2)}, u32[]{:S(2)}) collective-permute-start(bf16[528,128]{1,0:T(8,128)(2,1)S(1)} %fusion.7), channel_id=1, source_target_pairs={{0,4},{4,0},{8,12},{12,8},{16,20},{20,16},{24,28},{28,24},{1,5},{5... | collective-permute-start | bytes 405512 | tf_op jit(solution)/shard_map/ppermute | solution.py:395
  52.8 3.6 %collective-permute-start.15 = (f32[2,512]{1,0:T(2,128)S(1)}, f32[2,512]{1,0:T(2,128)S(1)}, u32[]{:S(2)}, u32[]{:S(2)}) collective-permute-start(f32[2,512]{1,0:T(2,128)S(1)} %broadcast_select_fusion), channel_id=1, source_target_pairs={{0,2},{1,3},{2,0},{3,1},{4,6},{5,7},{6,4},{7,5},{8,10},{9,11},{10,... | collective-permute-start | bytes 12296 | tf_op jit(solution)/shard_map/ppermute | solution.py:395
